TPU v7x, 512 devices: a whole 4x8x8 slice. The times are simulated.
512 devices in a mesh: seq: 64 (over y, x, core), res: 8 (over z).
Axes of the slice: x: 4, y: 8, z: 8, core: 2. Of those that a mesh axis runs over, the one named last changes fastest.
Arguments:
- alignment: bfloat16 [128, 512, 64], P('seq', 'res'), may hold values from -16 to 16
- cotangent: bfloat16 [128, 512, 64], P('seq', 'res'), may hold values from -6 to 6
- pair_bias: bfloat16 [8, 512, 512], P(None, 'res'), may hold values from -8 to 360
- norm_gains: float32 [2, 64], replicated, may hold values from 0.5 to 1.5
- row_project: float32 [64, 256], replicated, may hold values from -0.75 to 0.75
- row_output: float32 [64, 64], replicated, may hold values from -0.75 to 0.75
- column_project: float32 [64, 144], replicated, may hold values from -16 to 16
- column_output: float32 [64, 64], replicated, may hold values from -0.75 to 0.75
- residue_mask: int32 [512], P('res'), may hold values 0 or 1
- sequence_mask: int32 [128], P('seq'), may hold values from 0 to 1, as said below
Outputs:
- grad_alignment: bfloat16 [128, 512, 64], P('seq', 'res')
- grad_pair_bias: float32 [8, 512, 512], P(None, 'res', 'seq')
- grad_gains: float32 [2, 64], replicated
- grad_row_project: float32 [64, 256], replicated
- grad_row_output: float32 [64, 64], replicated
- grad_column_project: float32 [64, 144], replicated
- grad_column_output: float32 [64, 64], replicated
Inputs may be any that keep to these rules, and one draw needn't show every extreme that they name: `sequence_mask`: at least one extra sequence is present.
All inputs are finite; a program needn't handle non-finite values. No bound on the sum of `residue_mask` on one device may be relied on, other than what follows from the above.
Results may differ from a plain program's by a relative error of at most 0.0027.
Values sent between devices are 32-bit elements; how exact they have to be, the bound alone decides.
A program may use at most 128 MiB of HBM per device.

v0:
```python
import jax
import jax.numpy as jnp
from jax import lax
from jax.sharding import PartitionSpec as P

C = 64
H = 8
DH = 8


PRECISE = lax.Precision.HIGHEST
EPSILON = 1e-05
MASKED = 1000000000.0


def layer_norm(values, gain_vector):
    centre = jnp.mean(values, axis=-1, keepdims=True)
    centred = values - centre
    spread = jnp.mean(centred * centred, axis=-1, keepdims=True)
    return centred * lax.rsqrt(spread + EPSILON) * gain_vector


def split_heads(memory):
    key_rows = memory[:, :C].reshape(memory.shape[0], H, DH)
    value_rows = memory[:, C:].reshape(memory.shape[0], H, DH)
    return (key_rows, value_rows)


def row_softmax(queries, key_rows, bias_block, key_bias):
    scores = (
        jnp.einsum("qhd,khd->hqk", queries, key_rows, precision=PRECISE)
        + bias_block
        + key_bias[None, None, :]
    )
    peak_value = jnp.max(scores, axis=-1, keepdims=True)
    exponent = jnp.exp(scores - peak_value)
    return exponent / jnp.sum(exponent, axis=-1, keepdims=True)


def column_moments(exponent, value_col):
    total_exp = jnp.sum(exponent, axis=0)
    weighted = jnp.einsum("srh,srd->rhd", exponent, value_col, precision=PRECISE)
    return (total_exp, weighted)


def local(
    alignment,
    cotangent,
    pair_bias,
    norm_gains,
    row_project,
    row_output,
    column_project,
    column_output,
    residue_mask,
    sequence_mask,
):
    sequence_count = alignment.shape[0]
    residue_count = alignment.shape[1]
    scaling = DH ** (-0.5)
    initial = alignment.astype(jnp.float32)
    key_bias = MASKED * (residue_mask.astype(jnp.float32) - 1.0)
    normed_row, row_backward = jax.vjp(layer_norm, initial, norm_gains[0])
    query_weights = jnp.concatenate([row_project[:, :C], row_project[:, 3 * C :]], axis=1)
    query_gate = jnp.einsum("src,cd->srd", normed_row, query_weights, precision=PRECISE)
    memory_weights = row_project[:, C : 3 * C]
    memory_local = jnp.einsum("src,cd->srd", normed_row, memory_weights, precision=PRECISE)
    memory_all, bias_all = (
        lax.all_gather(memory_local, "res", axis=1, tiled=True),
        lax.all_gather(key_bias, "res", axis=0, tiled=True),
    )
    queries_row = (query_gate[..., :C] * scaling).reshape(sequence_count, residue_count, H, DH)
    gate_row = jax.nn.sigmoid(query_gate[..., C:])

    def mix_single(members):
        queries, memory = members
        key_rows, value_rows = split_heads(memory)
        weights = row_softmax(queries, key_rows, pair_bias, bias_all)
        return jnp.einsum("hqk,khd->qhd", weights, value_rows, precision=PRECISE).reshape(-1, C)

    mixture_row = lax.map(mix_single, (queries_row, memory_all))
    middle = initial + jnp.einsum(
        "src,cd->srd", gate_row * mixture_row, row_output, precision=PRECISE
    )
    present = sequence_mask.astype(jnp.float32)
    normed_col, col_backward = jax.vjp(layer_norm, middle, norm_gains[1])
    gate_col = jax.nn.sigmoid(
        jnp.einsum("src,cd->srd", normed_col, column_project[:, C + 2 * DH :], precision=PRECISE)
    )
    grad_top = cotangent.astype(jnp.float32)
    grad_gate_col = jnp.einsum("srd,cd->src", grad_top, column_output, precision=PRECISE)
    local_sum = jnp.einsum("s,src->rc", present, normed_col, precision=PRECISE)
    gated_local = jnp.sum(gate_col * grad_gate_col, axis=0)
    total_sum, counted, grad_mixture_col = lax.psum(
        (local_sum, jnp.sum(present), gated_local), "seq"
    )
    mean_normed = total_sum / counted
    queries_col = (
        jnp.dot(mean_normed, column_project[:, :C], precision=PRECISE) * scaling
    ).reshape(residue_count, H, DH)
    key_value_col = jnp.einsum(
        "src,cd->srd", normed_col, column_project[:, C : C + 2 * DH], precision=PRECISE
    )
    key_col = key_value_col[..., :DH]
    value_col = key_value_col[..., DH:]
    scores_col = (
        jnp.einsum("rhd,srd->srh", queries_col, key_col, precision=PRECISE)
        + MASKED * (present - 1.0)[:, None, None]
    )
    peak_col = lax.pmax(jnp.max(scores_col, axis=0), "seq")
    exponent_col = jnp.exp(scores_col - peak_col[None])
    local_exp, local_packed = column_moments(exponent_col, value_col)
    totals_exp, totals_packed = lax.psum((local_exp, local_packed), "seq")
    mixture_col = totals_packed / totals_exp[..., None]
    weights_col = exponent_col / totals_exp[None]
    mixture_flat = mixture_col.reshape(residue_count, C)
    grad_col_output = jnp.einsum(
        "src,srd->cd", gate_col * mixture_flat[None], grad_top, precision=PRECISE
    )
    grad_gate_pre = grad_gate_col * mixture_flat[None] * gate_col * (1.0 - gate_col)
    grad_heads_col = grad_mixture_col.reshape(residue_count, H, DH)
    grad_weights_col = jnp.einsum("rhd,srd->srh", grad_heads_col, value_col, precision=PRECISE)
    inner_dot = jnp.sum(grad_heads_col * mixture_col, axis=-1)
    grad_scores_col = weights_col * (grad_weights_col - inner_dot[None])
    grad_key_col = jnp.einsum("srh,rhd->srd", grad_scores_col, queries_col, precision=PRECISE)
    grad_value_col = jnp.einsum("srh,rhd->srd", weights_col, grad_heads_col, precision=PRECISE)
    grad_key_value = jnp.concatenate([grad_key_col, grad_value_col], axis=-1)
    grad_queries = lax.psum(
        jnp.einsum("srh,srd->rhd", grad_scores_col, key_col, precision=PRECISE), "seq"
    )
    grad_query_flat = grad_queries.reshape(residue_count, C) * scaling
    grad_mean = jnp.dot(grad_query_flat, column_project[:, :C].T, precision=PRECISE)
    grad_col_project = jnp.concatenate(
        [
            jnp.dot((local_sum / counted).T, grad_query_flat, precision=PRECISE),
            jnp.einsum("src,srd->cd", normed_col, grad_key_value, precision=PRECISE),
            jnp.einsum("src,srd->cd", normed_col, grad_gate_pre, precision=PRECISE),
        ],
        axis=1,
    )
    grad_normed_col = present[:, None, None] / counted * grad_mean[None]
    grad_normed_col = grad_normed_col + jnp.einsum(
        "srd,cd->src", grad_key_value, column_project[:, C : C + 2 * DH], precision=PRECISE
    )
    grad_normed_col = grad_normed_col + jnp.einsum(
        "srd,cd->src", grad_gate_pre, column_project[:, C + 2 * DH :], precision=PRECISE
    )
    grad_middle_norm, grad_gain_col = col_backward(grad_normed_col)
    grad_middle = grad_top + grad_middle_norm
    grad_gate_row = jnp.einsum("srd,cd->src", grad_middle, row_output, precision=PRECISE)
    grad_row_output = jnp.einsum(
        "src,srd->cd", gate_row * mixture_row, grad_middle, precision=PRECISE
    )
    grad_row_pre = grad_gate_row * mixture_row * gate_row * (1.0 - gate_row)
    grad_mixture_row = grad_gate_row * gate_row

    def back_single(accumulated, members):
        queries, memory, grad_mixed = members
        key_rows, value_rows = split_heads(memory)
        weights = row_softmax(queries, key_rows, pair_bias, bias_all)
        grad_heads = grad_mixed.reshape(-1, H, DH)
        grad_weights = jnp.einsum("qhd,khd->hqk", grad_heads, value_rows, precision=PRECISE)
        inner_row = jnp.sum(weights * grad_weights, axis=-1, keepdims=True)
        grad_scores = weights * (grad_weights - inner_row)
        grad_query = jnp.einsum("hqk,khd->qhd", grad_scores, key_rows, precision=PRECISE).reshape(
            -1, C
        )
        grad_key = jnp.einsum("hqk,qhd->khd", grad_scores, queries, precision=PRECISE).reshape(
            -1, C
        )
        grad_value = jnp.einsum("hqk,qhd->khd", weights, grad_heads, precision=PRECISE).reshape(
            -1, C
        )
        return (
            accumulated + grad_scores,
            (grad_query, jnp.concatenate([grad_key, grad_value], axis=1)),
        )

    start_bias = jnp.zeros(pair_bias.shape, jnp.float32)
    bias_part, (grad_query_rows, grad_memory_all) = lax.scan(
        back_single, start_bias, (queries_row, memory_all, grad_mixture_row)
    )
    grad_memory = lax.psum_scatter(grad_memory_all, "res", scatter_dimension=1, tiled=True)
    grad_memory_weights = jnp.einsum("src,srd->cd", normed_row, grad_memory, precision=PRECISE)
    grad_from_keys = jnp.einsum("srd,cd->src", grad_memory, memory_weights, precision=PRECISE)
    grad_query_scaled = grad_query_rows * scaling
    grad_row_project = jnp.concatenate(
        [
            jnp.einsum("src,srd->cd", normed_row, grad_query_scaled, precision=PRECISE),
            grad_memory_weights,
            jnp.einsum("src,srd->cd", normed_row, grad_row_pre, precision=PRECISE),
        ],
        axis=1,
    )
    grad_normed_row = grad_from_keys + jnp.einsum(
        "srd,cd->src", grad_query_scaled, row_project[:, :C], precision=PRECISE
    )
    grad_normed_row = grad_normed_row + jnp.einsum(
        "srd,cd->src", grad_row_pre, row_project[:, 3 * C :], precision=PRECISE
    )
    grad_initial, grad_gain_row = row_backward(grad_normed_row)
    grad_alignment = (grad_middle + grad_initial).astype(jnp.bfloat16)
    grad_pair_bias = lax.psum_scatter(bias_part, "seq", scatter_dimension=2, tiled=True)
    grad_gains, summed_row_project, summed_row_output, summed_col_project, summed_col_output = (
        lax.psum(
            (
                jnp.stack([grad_gain_row, grad_gain_col]),
                grad_row_project,
                grad_row_output,
                grad_col_project,
                grad_col_output,
            ),
            ("seq", "res"),
        )
    )
    return (
        grad_alignment,
        grad_pair_bias,
        grad_gains,
        summed_row_project,
        summed_row_output,
        summed_col_project,
        summed_col_output,
    )


def solution(mesh):
    placed = (
        P("seq", "res", None),
        P("seq", "res", None),
        P(None, "res", None),
        P(),
        P(),
        P(),
        P(),
        P(),
        P("res"),
        P("seq"),
    )
    return jax.shard_map(
        local,
        mesh=mesh,
        in_specs=placed,
        out_specs=(P("seq", "res", None), P(None, "res", "seq"), P(), P(), P(), P(), P()),
        check_vma=False,
    )
```

profile of v0, /device:TPU:1, one launch (start us, length us, event | category | flops | bytes accessed | tf_op | source)
XLA Modules:
  0.0 1722.9 jit_solution(11042458780904640257)
XLA Ops:
  8.1 1.3 convert_reduce_fusion.1
  9.4 0.8 slice_bitcast_fusion.9
  10.2 1.4 fusion.134
  12.2 0.8 multiply_dynamic-update-slice_fusion
  12.9 20.2 %all-reduce = f32[512]{0:T(512)S(1)} all-reduce(f32[512]{0:T(512)S(1)} %multiply_dynamic-update-slice_fusion), channel_id=1, replica_groups=mesh['seq'=64,'res'=8] {'res'}, use_global_device_ids=true, to_apply=%add | all-reduce | flops 512 | bytes 4096
  33.2 0.8 copy.131
  34.1 0.8 copy.130
  35.0 1.0 fusion.63
  36.0 0.9 fusion.132
  36.9 1.2 fusion.36
  38.5 19.4 %all_gather.6 = f32[2,512,128]{2,1,0:T(8,128)S(1)} all-gather(f32[2,64,128]{2,1,0:T(8,128)S(1)} %fusion.36), channel_id=1, replica_groups=mesh['seq'=64,'res'=8] {'res'}, dimensions={1}, use_global_device_ids=true | all-gather | bytes 589824 | tf_op jit(solution)/shard_map/all_gather | solution.py:69
  58.2 5.6 while.25
  58.2 1.2 fusion.168
  59.8 1.1 convolution_bitcast_fusion.17
  61.0 1.2 fusion.168
  62.6 1.1 convolution_bitcast_fusion.17
  65.8 251.9 %all-reduce.4 = (f32[64,64]{1,0:T(8,128)S(1)}, f32[]{:T(128)}) all-reduce(f32[64,64]{1,0:T(8,128)S(1)} %bitcast.212, f32[]{:T(128)} %convert_reduce_fusion.1), channel_id=1, replica_groups=mesh['seq'=64,'res'=8] {'seq'}, use_global_device_ids=true, to_apply=%region_10.11 | all-reduce | flops 4097 | bytes 32776 | tf_op jit(solution)/shard_map/psum | solution.py:94
  317.7 1.2 convert_divide_fusion
  318.9 0.8 convolution_multiply_fusion
  321.0 246.1 %pmax.7 = f32[64,8]{1,0:T(8,128)S(1)} all-reduce(f32[64,8]{1,0:T(8,128)S(1)} %get-tuple-element.279), channel_id=1, replica_groups=mesh['seq'=64,'res'=8] {'seq'}, use_global_device_ids=true, to_apply=%region_12.13 | all-reduce | flops 512 | bytes 4096 | tf_op jit(solution)/shard_map/pmax | solution.py:110
  567.4 0.7 fusion.121
  568.1 252.1 %all-reduce.3 = (f32[64,8,8]{2,1,0:T(8,128)S(1)}, f32[64,8,8]{2,1,0:T(8,128)S(1)}, f32[64,8]{1,0:T(8,128)S(1)}) all-reduce(f32[64,8,8]{2,1,0:T(8,128)S(1)} %copy.145, f32[64,8,8]{2,1,0:T(8,128)S(1)} %fusion.121, f32[64,8]{1,0:T(8,128)S(1)} %fusion.122), channel_id=1, replica_groups=mesh['seq'=64,'res'=8] {'seq'}, use_global_device_ids=true, to_apply=%region_16.17 | all-reduce | flops 8704 | bytes 69632 | tf_op jit(solution)/shard_map/psum | solution.py:94
  822.2 0.7 fusion.137
  823.4 246.4 %psum.82 = f32[64,8,8]{0,2,1:T(8,128)S(1)} all-reduce(f32[64,8,8]{0,2,1:T(8,128)S(1)} %copy.149), channel_id=1, replica_groups=mesh['seq'=64,'res'=8] {'seq'}, use_global_device_ids=true, to_apply=%region_19.20 | all-reduce | flops 4096 | bytes 32768 | tf_op jit(solution)/shard_map/psum | solution.py:128
  1070.0 0.9 convolution_add_fusion.5
  1070.9 1.7 multiply_reduce_fusion.2
  1072.8 0.9 fusion.125
  1073.7 0.6 broadcast.120.clone
  1074.4 29.6 %while.26 = (s32[]{:T(128)}, f32[8,64,512]{2,1,0:T(8,128)S(1)}, f32[2,64,64]{2,1,0:T(8,128)}, f32[2,512,128]{2,0,1:T(2,128)}, f32[2,64,8,8]{1,3,2,0:T(8,128)S(1)...) while((s32[]{:T(128)}, f32[8,64,512]{2,1,0:T(8,128)S(1)}, ...), condition=%wide.region_26.27_spmd.clone, body=%wide.region_22.0_spmd.clone.sunk | while | flops 130611712 | bytes 16429263 | solution.py:180
  1075.1 1.2 fusion.175
  1076.7 0.8 convolution_bitcast_fusion.19
  1077.5 1.2 multiply_reduce_fusion.7
  1079.3 1.0 convolution_bitcast_fusion.18
  1080.3 0.6 constant_dynamic-update-slice_fusion.5
  1080.9 0.6 convolution_bitcast_fusion.20
  1081.7 7.5 dynamic_update_slice.20
  1089.2 0.6 copy-done.7
  1089.9 1.2 fusion.175
  1091.5 0.8 convolution_bitcast_fusion.19
  1092.3 1.2 multiply_reduce_fusion.7
  1094.1 1.0 convolution_bitcast_fusion.18
  1095.1 0.6 constant_dynamic-update-slice_fusion.5
  1095.7 0.6 convolution_bitcast_fusion.20
  1096.5 7.5 dynamic_update_slice.20
  1104.2 0.9 convolution_bitcast_fusion.8
  1105.1 1.1 convolution_bitcast_fusion.7
  1106.2 1.7 fusion.59
  1107.9 0.7 pad_maximum_fusion.1
  1109.2 1.1 convolution_bitcast_fusion.12
  1110.4 1.7 convolution_bitcast_fusion.6
  1112.1 1.9 convolution_bitcast_fusion.9
  1114.0 1.2 convolution_bitcast_fusion.10
  1115.2 63.3 %all-reduce.11.cloned.1.call-done = f32[2,512,128]{2,0,1:T(2,128)} async-done(((f32[2,512,128]{2,0,1:T(2,128)}), f32[2,512,128]{2,0,1:T(2,128)}) %all-reduce.11.cloned.1.call-update) | async-done | bytes 524304
  1178.6 0.8 constant_dynamic-slice_fusion.1
  1180.9 0.7 pad_maximum_fusion
  1182.5 2.0 copy.163
  1184.6 0.7 copy.170
  1185.3 261.0 %all-reduce.9.cloned.1.call-done = f32[64,256]{1,0:T(8,128)} async-done(((f32[64,256]{1,0:T(8,128)}), f32[64,256]{1,0:T(8,128)}) %all-reduce.9.cloned.1.call-update) | async-done | bytes 65552 | tf_op jit(solution)/shard_map/psum | solution.py:205
  1446.3 262.6 %all-reduce.13.cloned.1.call-done = (f32[2,64]{1,0:T(2,128)}, f32[64,64]{1,0:T(8,128)}, f32[64,144]{1,0:T(8,128)}, f32[64,64]{1,0:T(8,128)}) async-done(((f32[2,64]{1,0:T(2,128)}, f32[64,64]{1,0:T(8,128)}, f32[64,144]{1,0:T(8,128)}, f32[64,64]{1,0:T(8,128)}), (f32[2,64]{1,0:T(2,128)}, f32[64,64]{1,0:T(8,128)}, f32[64,144]{1,0:T(8,128)}, f32[64,64]{1,0:T(8,128)})) %all-reduce.13.cloned.1.call-update) | async-done | bytes 70160 | tf_op jit(solution)/shard_map/psum | solution.py:205
  1708.9 1.2 copy.249
  1710.1 1.5 copy.250
  1711.6 1.4 copy.251
  1712.9 1.5 copy.252
  1714.4 1.4 copy.253
  (168 shorter events, 13.4 us)
Async XLA Ops:
  8.0 55.8 %copy-start = (f32[64,64]{1,0:T(8,128)S(1)}, f32[64,64]{1,0:T(8,128)}, u32[]{:S(2)}) copy-start(f32[64,64]{1,0:T(8,128)} %param.19) | copy-start | bytes 49156
  8.0 50.1 %copy-start.1 = (bf16[8,64,512]{2,1,0:T(8,128)(2,1)S(1)}, bf16[8,64,512]{2,1,0:T(8,128)(2,1)}, u32[]{:S(2)}) copy-start(bf16[8,64,512]{2,1,0:T(8,128)(2,1)} %param.16) | copy-start | bytes 1572868
  8.0 1170.5 %all-reduce.11.cloned.1.call-start = ((), (), s32[]{:S(2)}) async-start(), calls=%async_computation.3 | async-start | bytes 1048576
  10.2 48.0 %copy-start.25 = (f32[64]{0:T(128)}, f32[64]{0:T(128)S(1)}, u32[]{:S(2)}) copy-start(f32[64]{0:T(128)S(1)} %get-tuple-element.272) | copy-start | bytes 772
  10.2 54.2 %copy-start.33 = (f32[64]{0:T(128)}, f32[64]{0:T(128)S(1)}, u32[]{:S(2)}) copy-start(f32[64]{0:T(128)S(1)} %get-tuple-element.271) | copy-start | bytes 772
  34.1 0.9 copy-start.31
  34.1 24.1 %copy-start.20 = (f32[2,64]{1,0:T(2,128)}, f32[2,64]{1,0:T(2,128)S(1)}, u32[]{:S(2)}) copy-start(f32[2,64]{1,0:T(2,128)S(1)} %fusion.107) | copy-start | bytes 1540
  35.0 1037.8 %copy-start.14 = (bf16[2,64,64]{1,2,0:T(8,128)(2,1)}, bf16[2,64,64]{1,2,0:T(8,128)(2,1)S(1)}, u32[]{:S(2)}) copy-start(bf16[2,64,64]{1,2,0:T(8,128)(2,1)S(1)} %copy.130) | copy-start | bytes 49156
  36.0 1034.9 %copy-start.3 = (f32[2,64,64]{2,1,0:T(8,128)}, f32[2,64,64]{2,1,0:T(8,128)S(1)}, u32[]{:S(2)}) copy-start(f32[2,64,64]{2,1,0:T(8,128)S(1)} %fusion.63) | copy-start | bytes 98308
  38.4 1034.4 %copy-start.12 = (f32[2,64,128]{2,1,0:T(8,128)}, f32[2,64,128]{2,1,0:T(8,128)S(1)}, u32[]{:S(2)}) copy-start(f32[2,64,128]{2,1,0:T(8,128)S(1)} %fusion.38) | copy-start | bytes 196612
  58.1 6.8 copy-start.11
  58.1 7.3 copy-start.38
  63.8 0.6 copy-start.18
  64.2 0.6 copy-start.23
  64.3 0.6 copy-start.29
  64.3 0.6 copy-start.27
  65.8 254.3 %copy-start.22 = (f32[1,64,64]{2,0,1:T(1,128)}, f32[1,64,64]{2,0,1:T(1,128)S(1)}, u32[]{:S(2)}) copy-start(f32[1,64,64]{2,0,1:T(1,128)S(1)} %fusion.109) | copy-start | bytes 49156
  320.1 750.7 %copy-start.4 = (f32[2,64,64]{2,1,0:T(8,128)}, f32[2,64,64]{2,1,0:T(8,128)S(1)}, u32[]{:S(2)}) copy-start(f32[2,64,64]{2,1,0:T(8,128)S(1)} %get-tuple-element.278) | copy-start | bytes 98308
  821.1 251.6 %copy-start.30 = (f32[2,64]{1,0:T(2,128)S(1)}, f32[2,64]{1,0:T(2,128)}, u32[]{:S(2)}) copy-start(f32[2,64]{1,0:T(2,128)} %copy-done.29) | copy-start | bytes 1540
  821.1 251.6 %copy-start.24 = (f32[2,64]{1,0:T(2,128)S(1)}, f32[2,64]{1,0:T(2,128)}, u32[]{:S(2)}) copy-start(f32[2,64]{1,0:T(2,128)} %copy-done.23) | copy-start | bytes 1540
  821.1 251.6 %copy-start.28 = (f32[2,64]{1,0:T(2,128)S(1)}, f32[2,64]{1,0:T(2,128)}, u32[]{:S(2)}) copy-start(f32[2,64]{1,0:T(2,128)} %copy-done.27) | copy-start | bytes 1540
  821.1 251.6 %copy-start.34 = (f32[64]{0:T(128)S(1)}, f32[64]{0:T(128)}, u32[]{:S(2)}) copy-start(f32[64]{0:T(128)} %copy-done.33) | copy-start | bytes 772
  823.1 251.3 %copy-start.17 = (f32[2,64,8]{1,2,0:T(8,128)}, f32[2,64,8]{1,2,0:T(8,128)S(1)}, u32[]{:S(2)}) copy-start(f32[2,64,8]{1,2,0:T(8,128)S(1)} %copy.153) | copy-start | bytes 12292
  823.3 251.1 %copy-start.5 = (f32[64,64]{1,0:T(8,128)}, f32[64,64]{1,0:T(8,128)S(1)}, u32[]{:S(2)}) copy-start(f32[64,64]{1,0:T(8,128)S(1)} %copy.155) | copy-start | bytes 49156
  1069.8 4.6 copy-start.16
  1072.8 1.6 copy-start.9
  1072.8 1.6 copy-start.35
  1074.4 0.6 copy-start.7
  1080.9 8.3 copy-start.8
  1089.2 0.6 copy-start.7
  1095.7 8.3 copy-start.8
  1104.0 75.4 %copy-start.21 = (f32[2,64]{1,0:T(2,128)S(1)}, f32[2,64]{1,0:T(2,128)}, u32[]{:S(2)}) copy-start(f32[2,64]{1,0:T(2,128)} %copy-done.20) | copy-start | bytes 1540
  1104.0 75.4 %copy-start.26 = (f32[64]{0:T(128)S(1)}, f32[64]{0:T(128)}, u32[]{:S(2)}) copy-start(f32[64]{0:T(128)} %copy-done.25) | copy-start | bytes 772
  1104.0 75.7 %copy-start.6 = (f32[64,256]{1,0:T(8,128)S(1)}, f32[64,256]{1,0:T(8,128)}, u32[]{:S(2)}) copy-start(f32[64,256]{1,0:T(8,128)} %param.18) | copy-start | bytes 196612
  1104.0 76.0 %copy-start.2 = (f32[2,64,64]{2,1,0:T(8,128)S(1)}, f32[2,64,64]{2,1,0:T(8,128)}, u32[]{:S(2)}) copy-start(f32[2,64,64]{2,1,0:T(8,128)} %get-tuple-element.90) | copy-start | bytes 98308
  1104.0 76.4 %copy-start.13 = (f32[2,64,128]{2,1,0:T(8,128)S(1)}, f32[2,64,128]{2,1,0:T(8,128)}, u32[]{:S(2)}) copy-start(f32[2,64,128]{2,1,0:T(8,128)} %copy-done.12) | copy-start | bytes 196612
  1104.0 76.4 %copy-start.19 = (f32[2,64,64]{2,1,0:T(8,128)S(1)}, f32[2,64,64]{2,1,0:T(8,128)}, u32[]{:S(2)}) copy-start(f32[2,64,64]{2,1,0:T(8,128)} %copy-done.18) | copy-start | bytes 98308
  1104.1 76.4 %copy-start.39 = (f32[2,64,64]{2,1,0:T(8,128)S(1)}, f32[2,64,64]{2,1,0:T(8,128)}, u32[]{:S(2)}) copy-start(f32[2,64,64]{2,1,0:T(8,128)} %get-tuple-element.283) | copy-start | bytes 98308
  1104.1 76.8 %copy-start.32 = (f32[2,64]{1,0:T(2,128)S(1)}, f32[2,64]{1,0:T(2,128)}, u32[]{:S(2)}) copy-start(f32[2,64]{1,0:T(2,128)} %copy-done.31) | copy-start | bytes 1540
  1104.1 77.7 %copy-start.37 = (f32[64]{0:T(128)S(1)}, f32[64]{0:T(128)}, u32[]{:S(2)}) copy-start(f32[64]{0:T(128)} %get-tuple-element.210) | copy-start | bytes 772
  1104.1 342.2 %all-reduce.9.cloned.1.call-start = ((), (), s32[]{:S(2)}) async-start(), calls=%async_computation.2 | async-start | bytes 131072 | tf_op jit(solution)/shard_map/psum | solution.py:205
  1181.6 527.2 %all-reduce.13.cloned.1.call-start = ((), (), s32[]{:S(2)}) async-start(), calls=%async_computation.4 | async-start | bytes 264192 | tf_op jit(solution)/shard_map/psum | solution.py:205
  1182.4 526.5 %reduce-scatter.2.cloned.1.call-start = ((), (), s32[]{:S(2)}) async-start(), calls=%async_computation.1 | async-start | bytes 2129920 | tf_op jit(solution)/shard_map/reduce_scatter | solution.py:203
  1182.5 2.0 copy-start.10
  1182.5 2.0 copy-start.15
  1182.5 2.0 copy-start.36
Sparse Core Ops, SparseCore 0:
  1104.2 74.2 all-reduce.10
  1184.1 262.1 all-reduce.8
  1453.5 255.2 all-reduce.12
Sparse Core Ops, SparseCore 1:
  1188.8 146.0 reduce-scatter.1
where the time goes:
time: 1730 us; the launch traced here: 1720 us
  blocking collectives  1040 us (60%)
  waiting for transfers between devices  587 us (34%)
  matrix products  37.3 us (2%)
  local copies, waits for them, and re-layouts  36.2 us (2%)
  between operations  17.3 us (1%)
    psum x2, waiting for transfers between devices, local(): lax.psum((jnp.stack([grad_gain_row, grad_gain_col]), grad_row_project, gr...  524 us
    psum x2, blocking collectives, local(): lax.psum((local_sum, jnp.sum(present), gated_local), 'seq')  504 us
    psum x1, blocking collectives, local(): lax.psum(jnp.einsum('srh,srd->rhd', grad_scores_col, key_col, precision=P...  246 us
    pmax x1, blocking collectives, local(): peak_col = lax.pmax(jnp.max(scores_col, axis=0), 'seq')  246 us
    unnamed x5, waiting for transfers between devices  63.4 us
  transfers between devices with their start and end apart: 4, of which 3 were waited for; matrix products, arithmetic and copies ran while one was open for 1% of the time, Pallas kernels for 0%

commit v1 on v0

v1 whole, which is shorter than its diff:
```python
import functools
import jax
import jax.numpy as jnp
from jax import lax
from jax.experimental import pallas as pl
from jax.experimental.pallas import tpu as pltpu
from jax.sharding import PartitionSpec as P

C = 64
H = 8
DH = 8
L = 2
PAIRS = 4
W = 128
EPSILON = 1e-05
MASKED = 1000000000.0
F32 = jnp.float32
BF16 = jnp.bfloat16
MESH = pl.DeviceIdType.MESH
NN = (((1,), (0,)), ((), ()))
NT = (((1,), (1,)), ((), ()))
TN = (((0,), (0,)), ((), ()))


def dot(a, b, dims=NN):
    return lax.dot_general(
        a, b, dims, precision=lax.Precision.HIGHEST, preferred_element_type=F32
    )


def dot1(a, b, dims=NN):
    return lax.dot_general(a, b, dims, preferred_element_type=F32)


def split2(a):
    high = a.astype(BF16)
    return high, (a - high.astype(F32)).astype(BF16)


def split3(a):
    high = a.astype(BF16)
    rest = a - high.astype(F32)
    middle = rest.astype(BF16)
    return high, middle, (rest - middle.astype(F32)).astype(BF16)


def dot3(a, b, dims=NN):
    ah, al = split2(a)
    bh, bl = split2(b)
    return dot1(ah, bh, dims) + (dot1(ah, bl, dims) + dot1(al, bh, dims))


def iota(shape, axis):
    return lax.broadcasted_iota(jnp.int32, shape, axis)


def ones_where(condition):
    return jnp.where(condition, 1.0, 0.0).astype(F32)


def twice(row):
    return jnp.concatenate([row, row], axis=1)


def fold(row):
    return row + jnp.concatenate([row[:, C:], row[:, :C]], axis=1)


def block_diagonal(weights):
    zero = jnp.zeros_like(weights)
    return jnp.concatenate(
        [jnp.concatenate([weights, zero], axis=1), jnp.concatenate([zero, weights], axis=1)], axis=0
    )


def diagonal_sum(full):
    return full[:C, :C] + full[C:, C:]


def kernel(
    sizes,
    align_ref,
    cot_ref,
    bias_ref,
    gains_ref,
    rowp_ref,
    rowo_ref,
    colp_ref,
    colo_ref,
    rmask_ref,
    smask_ref,
    galign_ref,
    gbias_ref,
    ggains_ref,
    growp_ref,
    growo_ref,
    gcolp_ref,
    gcolo_ref,
    xall,
    gsend,
    grecv,
    msend,
    mrecv,
    bsend,
    brecv,
    bias_t,
    exps,
    bias_s,
    core_r,
    x_s,
    x_r,
    y_s,
    y_r,
    zr_s,
    zr_r,
    pc_s,
    pc_r,
    pr_s,
    pr_r,
    t_s,
    t_r,
    o_r,
    send_sem,
    recv_sem,
    bias_send,
    bias_recv,
):
    ny, nx, nz = sizes
    ns = ny * nx * 2
    res = ns
    keys = nz * res
    wide = 4 * res
    half = 2 * res
    block = keys // ns
    me = lax.axis_index("seq")
    mz = lax.axis_index("res")
    core = lax.rem(me, 2)
    mx = lax.rem(me // 2, nx)
    my = me // (2 * nx)
    scaling = DH ** (-0.5)

    barrier = pltpu.get_barrier_semaphore()

    def greet_seq(i, carry):
        pl.semaphore_signal(
            barrier, inc=1, device_id=(lax.rem(me + i, ns), mz), device_id_type=MESH
        )
        return carry

    def greet_res(i, carry):
        pl.semaphore_signal(
            barrier, inc=1, device_id=(me, lax.rem(mz + i, nz)), device_id_type=MESH
        )
        return carry

    lax.fori_loop(1, nz, greet_res, 0)
    lax.fori_loop(1, ns, greet_seq, 0)

    def to_seq(source, target, which):
        def one(i, carry):
            j = lax.rem(me + i, ns)
            pltpu.make_async_remote_copy(
                src_ref=source(j),
                dst_ref=target.at[me],
                send_sem=send_sem.at[which],
                recv_sem=recv_sem.at[which],
                device_id=(j, mz),
                device_id_type=MESH,
            ).start()
            return carry

        lax.fori_loop(1, ns, one, 0)

    def to_res(source, target, which):
        def one(i, carry):
            j = lax.rem(mz + i, nz)
            pltpu.make_async_remote_copy(
                src_ref=source(j),
                dst_ref=target.at[mz],
                send_sem=send_sem.at[which],
                recv_sem=recv_sem.at[which],
                device_id=(me, j),
                device_id_type=MESH,
            ).start()
            return carry

        lax.fori_loop(1, nz, one, 0)

    def wait(ref, semaphore):
        pltpu.make_async_copy(ref, ref, semaphore).wait()

    def wait_all(buffer, which, count):
        part = buffer.at[pl.ds(0, count - 1)]
        wait(part, recv_sem.at[which])
        wait(part, send_sem.at[which])

    def keep(source, target, at):
        target[pl.ds(at, 1)] = source[pl.ds(at, 1)]

    align = align_ref[...].astype(F32)
    initial = jnp.concatenate([align[0], align[1]], axis=1)
    cot = cot_ref[...].astype(F32)
    top_local = jnp.concatenate([cot[0], cot[1]], axis=1)
    gains = gains_ref[...]
    gain_row = twice(gains[0:1])
    gain_col = twice(gains[1:2])
    averaging = ones_where(iota((W, W), 0) // C == iota((W, W), 1) // C) * (1.0 / C)

    def layer_norm(values):
        centred = values - dot(values, averaging)
        spread = dot(centred * centred, averaging)
        inverse = lax.rsqrt(spread + EPSILON)
        return centred * inverse, inverse

    def layer_norm_back(grad_normed, gain, hat, inverse):
        scaled = grad_normed * gain
        rows = scaled.shape[0]
        means = dot(jnp.concatenate([scaled, scaled * hat], axis=0), averaging)
        return inverse * (scaled - means[:rows] - hat * means[rows:])

    hat_local, inverse_local = layer_norm(initial)
    xall[mz, 0:res, :] = hat_local
    xall[mz, res : res + 8, :] = jnp.broadcast_to(rmask_ref[...].astype(F32), (8, W))
    present_row = smask_ref[...].astype(F32)
    gsend[:, 0, 0:W] = top_local
    gsend[:, 0, W : 2 * W] = jnp.broadcast_to(present_row, (res, W))

    pl.semaphore_wait(barrier, ns + nz - 2)
    to_res(lambda j: xall.at[mz], xall, 0)
    to_seq(lambda j: gsend.at[j], grecv, 1)
    keep(gsend, grecv, me)

    lane = iota((C, W), 1)
    column = (lane // 32) * 16 + lane % 16
    chosen = [
        ones_where((iota((C, W), 0) == column) & ((lane // 16) % 2 == s)) for s in range(L)
    ]

    def spread_columns(weights):
        return jnp.concatenate([dot(weights, chosen[0]), dot(weights, chosen[1])], axis=0)

    def gather_columns(full):
        return dot(full[:C], chosen[0], NT) + dot(full[C:], chosen[1], NT)

    rowp = rowp_ref[...]
    query_w = spread_columns(rowp[:, 0:C])
    key_w = spread_columns(rowp[:, C : 2 * C])
    value_w = spread_columns(rowp[:, 2 * C : 3 * C])
    gate_w = spread_columns(rowp[:, 3 * C :])
    rowo = rowo_ref[...]
    out_w = jnp.concatenate([dot(chosen[0], rowo, TN), dot(chosen[1], rowo, TN)], axis=1)
    memory_w = jnp.concatenate([key_w, value_w], axis=1)

    normed_local = hat_local * gain_row
    queries = dot(normed_local, query_w) * scaling
    gate_row = jax.nn.sigmoid(dot(normed_local, gate_w))

    for p in range(PAIRS):
        pair = bias_ref[2 * p : 2 * p + 2].astype(F32).reshape(half, keys)
        bias_t[p] = pair.T

    match = iota((W, wide), 0) // DH - iota((W, wide), 1) // res

    def heads_apart(rows):
        flat = rows.T
        flat = jnp.concatenate([flat, flat, flat, flat], axis=1)
        return [jnp.where(match == 4 * p, flat, 0.0) for p in range(PAIRS)]

    queries_apart = heads_apart(queries)
    query_terms = []
    for p in range(PAIRS):
        q1, q2, q3 = split3(queries_apart[p])
        query_terms.append(
            (
                jnp.concatenate([q1, q1], axis=0),
                jnp.concatenate([q2, q2], axis=0),
                jnp.concatenate([q3, q1], axis=0),
            )
        )

    mine = ones_where(iota((32, wide), 0) // DH == iota((32, wide), 1) // res)

    def heads_together(apart):
        kept = apart * mine
        both = kept[:, :half] + kept[:, half:]
        return both[:, :res] + both[:, res:]

    colp = colp_ref[...]
    colo = colo_ref[...]
    entry = iota((C + 2 * DH + C, C), 0)
    entry_lane = iota((C + 2 * DH + C, C), 1)
    key_col_w = block_diagonal(dot(colp, ones_where(entry == C + entry_lane % DH)))
    value_col_w = block_diagonal(dot(colp, ones_where(entry == C + DH + entry_lane % DH)))
    gate_col_w = block_diagonal(dot(colp, ones_where(entry == C + 2 * DH + entry_lane)))
    query_col_w = block_diagonal(colp[:, 0:C])
    out_col_w = block_diagonal(colo)
    column_w = jnp.concatenate([key_col_w, value_col_w, gate_col_w], axis=1)
    head_sum = ones_where(iota((W, W), 0) // DH == iota((W, W), 1) // DH)

    wait_all(xall, 0, nz)
    hat_all = xall[:, 0:res, :].reshape(keys, W)
    normed_all = hat_all * gain_row
    memory = dot(normed_all, memory_w)
    key_rows = memory[:, :W]
    value_rows = memory[:, W:]
    value_flat = value_rows.T
    mask_flat = jnp.concatenate([xall[z, res : res + 8, :] for z in range(nz)], axis=0).T
    key_bias = jnp.concatenate(
        [MASKED * (mask_flat[:res, 8 * z : 8 * z + 1] - 1.0) for z in range(nz)], axis=0
    )
    k1, k2, k3 = split3(key_rows)
    k12 = jnp.concatenate([k1, k2], axis=1)
    k13 = jnp.concatenate([k1, k3], axis=1)
    value_high, value_low = split2(value_flat)

    totals = []
    mixed = []
    for p in range(PAIRS):
        terms = query_terms[p]
        scores = dot1(k12, terms[0]) + (dot1(k12, terms[1]) + dot1(k13, terms[2]))
        scores = scores + twice(bias_t[p]) + key_bias
        peak = jnp.max(scores, axis=0, keepdims=True)
        exponent = jnp.exp(scores - peak)
        exps[p] = exponent
        inverse_total = 1.0 / jnp.sum(exponent, axis=0, keepdims=True)
        totals.append(inverse_total)
        eh, el = split2(exponent)
        vh = value_high[32 * p : 32 * p + 32]
        vl = value_low[32 * p : 32 * p + 32]
        apart = dot1(vh, eh) + (dot1(vl, eh) + dot1(vh, el))
        mixed.append(heads_together(apart * inverse_total))
    mixture = jnp.concatenate(mixed, axis=0).T
    gated = gate_row * mixture
    middle = initial + dot(gated, out_w)
    msend[:, 0, :] = middle
    to_seq(lambda j: msend.at[j], mrecv, 2)
    keep(msend, mrecv, me)

    wait_all(grecv, 1, ns)
    top = grecv[:, 0, 0:W]
    present = grecv[:, 0, W : 2 * W]
    counted = jnp.sum(fold(jnp.sum(present, axis=0, keepdims=True)), axis=1, keepdims=True) * (
        1.0 / W
    )
    inverse_count = 1.0 / counted
    grad_gated_col = dot(top, out_col_w, NT)

    wait_all(mrecv, 2, ns)
    hat_col, inverse_col = layer_norm(mrecv[:, 0, :])
    normed_col = hat_col * gain_col
    mean_normed = fold(jnp.sum(present * normed_col, axis=0, keepdims=True)) * inverse_count
    queries_col = dot(mean_normed, query_col_w) * scaling
    projected = dot(normed_col, column_w)
    key_col = projected[:, 0:W]
    value_col = projected[:, W : 2 * W]
    gate_col = jax.nn.sigmoid(projected[:, 2 * W :])
    scores_col = dot(key_col * queries_col, head_sum) + MASKED * (present - 1.0)
    peak_row = jnp.max(scores_col, axis=0, keepdims=True)
    peak_row = jnp.maximum(peak_row, jnp.concatenate([peak_row[:, C:], peak_row[:, :C]], axis=1))
    exp_col = jnp.exp(scores_col - peak_row)
    weights_col = exp_col * (1.0 / fold(jnp.sum(exp_col, axis=0, keepdims=True)))
    mixture_col = fold(jnp.sum(weights_col * value_col, axis=0, keepdims=True))
    grad_mixture_col = fold(jnp.sum(gate_col * grad_gated_col, axis=0, keepdims=True))
    grad_gate_col = grad_gated_col * mixture_col * gate_col * (1.0 - gate_col)
    grad_weights_col = dot(value_col * grad_mixture_col, head_sum)
    inner_col = fold(jnp.sum(weights_col * grad_weights_col, axis=0, keepdims=True))
    grad_scores_col = weights_col * (grad_weights_col - inner_col)
    grad_query_col = fold(jnp.sum(grad_scores_col * key_col, axis=0, keepdims=True)) * scaling
    grad_key_col = grad_scores_col * queries_col
    grad_value_col = weights_col * grad_mixture_col
    grad_mean = dot(grad_query_col, query_col_w, NT)
    grad_projected = jnp.concatenate([grad_key_col, grad_value_col, grad_gate_col], axis=1)
    grad_normed_col = present * inverse_count * grad_mean + dot(grad_projected, column_w, NT)
    grad_middle_col = top + layer_norm_back(grad_normed_col, gain_col, hat_col, inverse_col)
    bsend[:, 0, :] = grad_middle_col
    to_seq(lambda j: bsend.at[j], brecv, 3)
    keep(bsend, brecv, me)

    pack_lane = iota((C, 2 * W), 1)
    pack_row = iota((C, 2 * W), 0)
    grad_full = dot(normed_col, grad_projected, TN)
    identity = ones_where(iota((C, C), 0) == iota((C, C), 1))
    mean_column = jnp.sum(identity * mean_normed[:, :C], axis=1, keepdims=True)
    grad_col_parts = jnp.concatenate(
        [
            mean_column * grad_query_col[:, :C],
            diagonal_sum(grad_full[:, 0:W]),
            diagonal_sum(grad_full[:, W : 2 * W]),
            diagonal_sum(grad_full[:, 2 * W :]),
            diagonal_sum(dot(gate_col * mixture_col, top, TN)),
        ],
        axis=1,
    )
    placing = jnp.concatenate(
        [
            ones_where(pack_lane == pack_row),
            ones_where(pack_lane == C + pack_row % DH),
            ones_where(pack_lane == C + DH + pack_row % DH),
            ones_where(pack_lane == C + 2 * DH + pack_row),
            ones_where(pack_lane == 2 * C + 2 * DH + pack_row),
        ],
        axis=0,
    )
    gain_sums = fold(jnp.sum(grad_normed_col * hat_col, axis=0, keepdims=True))
    gain_column = jnp.sum(identity * gain_sums[:, :C], axis=1, keepdims=True)
    pack = dot(grad_col_parts, placing) + jnp.where(
        pack_lane == 3 * C + 2 * DH, gain_column, 0.0
    )
    pc_s[...] = pack.reshape(ns, C // ns, 2 * W)
    to_seq(lambda j: pc_s.at[j], pc_r, 4)
    keep(pc_s, pc_r, me)

    key_flat = key_rows.T
    key_high, key_low = split2(key_flat)
    v1, v2 = split2(value_rows)
    v12 = jnp.concatenate([v1, v2], axis=1)

    wait_all(brecv, 3, ns)
    grad_middle = brecv[:, 0, :]
    grad_gated = dot(grad_middle, out_w, NT)
    grad_gate = grad_gated * mixture * gate_row * (1.0 - gate_row)
    grads_apart = heads_apart(grad_gated * gate_row)

    def bias_core(p):
        return pltpu.make_async_remote_copy(
            src_ref=bias_s.at[p, :, :, 1 - core],
            dst_ref=core_r.at[p],
            send_sem=bias_send.at[0, p],
            recv_sem=bias_recv.at[0, p],
            device_id=(me + 1 - 2 * core, mz),
            device_id_type=MESH,
        )

    def bias_to_x(p):
        bias_core(p).wait()
        x_s[p] = jnp.swapaxes(bias_s[p, :, :, core] + core_r[p], 0, 1)

        def one(i, carry):
            j = lax.rem(mx + i, nx)
            pltpu.make_async_remote_copy(
                src_ref=x_s.at[p, j],
                dst_ref=x_r.at[p, mx],
                send_sem=bias_send.at[1, p],
                recv_sem=bias_recv.at[1, p],
                device_id=((my * nx + j) * 2 + core, mz),
                device_id_type=MESH,
            ).start()
            return carry

        lax.fori_loop(1, nx, one, 0)
        x_r[p, pl.ds(mx, 1)] = x_s[p, pl.ds(mx, 1)]

    def bias_to_y(p):
        part = x_r.at[p, pl.ds(0, nx - 1)]
        wait(part, bias_recv.at[1, p])
        wait(part, bias_send.at[1, p])
        y_s[p] = sum([x_r[p, i] for i in range(1, nx)], x_r[p, 0])

        def one(i, carry):
            j = lax.rem(my + i, ny)
            pltpu.make_async_remote_copy(
                src_ref=y_s.at[p, j],
                dst_ref=y_r.at[p, my],
                send_sem=bias_send.at[2, p],
                recv_sem=bias_recv.at[2, p],
                device_id=((j * nx + mx) * 2 + core, mz),
                device_id_type=MESH,
            ).start()
            return carry

        lax.fori_loop(1, ny, one, 0)
        y_r[p, pl.ds(my, 1)] = y_s[p, pl.ds(my, 1)]

    def bias_done(p):
        part = y_r.at[p, pl.ds(0, ny - 1)]
        wait(part, bias_recv.at[2, p])
        wait(part, bias_send.at[2, p])
        total = sum([y_r[p, i] for i in range(1, ny)], y_r[p, 0])
        flat = total.T
        gbias_ref[2 * p] = flat[:res]
        gbias_ref[2 * p + 1] = flat[res:]

    grad_keys = jnp.zeros((keys, W), F32)
    grad_values = jnp.zeros((keys, W), F32)
    grad_queries = []
    for p in range(PAIRS):
        gh, gl = split2(grads_apart[p])
        grad_weights = dot1(v12, jnp.concatenate([gh, gh], axis=0)) + dot1(v1, gl)
        weights = exps[p] * totals[p]
        inner = jnp.sum(weights * grad_weights, axis=0, keepdims=True)
        grad_scores = weights * (grad_weights - inner)
        bias_s[p] = (grad_scores[:, :half] + grad_scores[:, half:]).reshape(
            ny, nx, 2, block, half
        )
        bias_core(p).start()
        sh, sl = split2(grad_scores)
        wh, wl = split2(weights)
        q1, q2 = split2(queries_apart[p])
        grad_keys = grad_keys + (dot1(sh, q1, NT) + (dot1(sh, q2, NT) + dot1(sl, q1, NT)))
        grad_values = grad_values + (dot1(wh, gh, NT) + (dot1(wh, gl, NT) + dot1(wl, gh, NT)))
        kh = key_high[32 * p : 32 * p + 32]
        kl = key_low[32 * p : 32 * p + 32]
        grad_queries.append(
            heads_together(dot1(kh, sh) + (dot1(kl, sh) + dot1(kh, sl)))
        )
        if p >= 1:
            bias_to_x(p - 1)
        if p >= 2:
            bias_to_y(p - 2)

    grad_memory = jnp.concatenate([grad_keys, grad_values], axis=1)
    partial = dot3(grad_memory, memory_w, NT)
    zr_s[...] = partial.reshape(nz, res, W)
    to_res(lambda j: zr_s.at[j], zr_r, 5)
    keep(zr_s, zr_r, mz)
    bias_to_x(PAIRS - 1)

    grad_query = jnp.concatenate(grad_queries, axis=0).T * scaling
    own_grads = jnp.concatenate([grad_query, grad_gate], axis=1)
    own_weights = jnp.concatenate([query_w, gate_w], axis=1)
    own_normed_grad = dot(own_grads, own_weights, NT)
    grad_memory_w = dot3(normed_all, grad_memory, TN)
    grad_own_w = dot(normed_local, own_grads, TN)
    grad_out_w = dot(gated, grad_middle, TN)
    gain_sums_row = fold(
        jnp.sum(partial * hat_all, axis=0, keepdims=True)
        + jnp.sum(own_normed_grad * hat_local, axis=0, keepdims=True)
    )
    gain_column_row = jnp.sum(identity * gain_sums_row[:, :C], axis=1, keepdims=True)
    grad_rowo = dot(chosen[0], grad_out_w[:, :C]) + dot(chosen[1], grad_out_w[:, C:])
    pack_row_part = jnp.concatenate(
        [
            gather_columns(grad_own_w[:, :W]),
            gather_columns(grad_memory_w[:, :W]),
            gather_columns(grad_memory_w[:, W:]),
            gather_columns(grad_own_w[:, W:]),
            grad_rowo,
            jnp.broadcast_to(gain_column_row, (C, C)),
        ],
        axis=1,
    )
    pr_s[...] = pack_row_part.reshape(ns, C // ns, 3 * W)
    to_seq(lambda j: pr_s.at[j], pr_r, 6)
    keep(pr_s, pr_r, me)
    bias_to_y(PAIRS - 2)

    wait_all(pc_r, 4, ns)
    wait_all(pr_r, 6, ns)
    t_s[...] = jnp.concatenate(
        [jnp.sum(pr_r[...], axis=0), jnp.sum(pc_r[...], axis=0)], axis=1
    )
    to_res(lambda j: t_s, t_r, 7)
    t_r[pl.ds(mz, 1)] = t_s[...][None]
    bias_to_y(PAIRS - 1)

    wait_all(zr_r, 5, nz)
    grad_normed_row = sum([zr_r[i] for i in range(1, nz)], zr_r[0]) + own_normed_grad
    grad_initial = layer_norm_back(grad_normed_row, gain_row, hat_local, inverse_local)
    grad_align = (grad_middle + grad_initial).astype(BF16)
    galign_ref[0] = grad_align[:, :C]
    galign_ref[1] = grad_align[:, C:]

    wait_all(t_r, 7, nz)
    o_r[me] = sum([t_r[i] for i in range(1, nz)], t_r[0])
    to_seq(lambda j: o_r.at[me], o_r, 8)
    for p in range(PAIRS):
        bias_done(p)
    wait_all(o_r, 8, ns)
    final = o_r[...].reshape(C, 5 * W)
    growp_ref[...] = final[:, 0 : 4 * C]
    growo_ref[...] = final[:, 4 * C : 5 * C]
    column_part = final[:, 3 * W :]
    gcolp_ref[...] = column_part[:, 0 : 2 * C + 2 * DH]
    gcolo_ref[...] = column_part[:, 2 * C + 2 * DH : 3 * C + 2 * DH]
    row_gain = final[:, 2 * W : 3 * W].T[C : C + 1]
    col_gain = column_part[:, W:].T[3 * C + 2 * DH - W : 3 * C + 2 * DH - W + 1]
    ggains_ref[0:1, :] = row_gain
    ggains_ref[1:2, :] = col_gain


def solution(mesh):
    seq_devices = mesh.shape["seq"]
    res_devices = mesh.shape["res"]
    nx = 4 if seq_devices == 64 else 2
    ny = seq_devices // (2 * nx)
    nz = res_devices
    res = seq_devices
    keys = nz * res
    block = keys // seq_devices
    half = 2 * res

    def local(
        alignment,
        cotangent,
        pair_bias,
        norm_gains,
        row_project,
        row_output,
        column_project,
        column_output,
        residue_mask,
        sequence_mask,
    ):
        rmask = jnp.pad(residue_mask[None], ((0, 0), (0, W - res)))
        smask = jnp.repeat(sequence_mask, C)[None]
        vmem = pl.BlockSpec(memory_space=pltpu.VMEM)
        ns = seq_devices
        chunk = C // ns
        return pl.pallas_call(
            functools.partial(kernel, (ny, nx, nz)),
            out_shape=(
                jax.ShapeDtypeStruct((L, res, C), BF16),
                jax.ShapeDtypeStruct((H, res, block), F32),
                jax.ShapeDtypeStruct((2, C), F32),
                jax.ShapeDtypeStruct((C, 4 * C), F32),
                jax.ShapeDtypeStruct((C, C), F32),
                jax.ShapeDtypeStruct((C, 2 * C + 2 * DH), F32),
                jax.ShapeDtypeStruct((C, C), F32),
            ),
            in_specs=[vmem] * 10,
            out_specs=(vmem,) * 7,
            scratch_shapes=[
                pltpu.VMEM((nz, res + 8, W), F32),
                pltpu.VMEM((ns, 1, 2 * W), F32),
                pltpu.VMEM((ns, 1, 2 * W), F32),
                pltpu.VMEM((ns, 1, W), F32),
                pltpu.VMEM((ns, 1, W), F32),
                pltpu.VMEM((ns, 1, W), F32),
                pltpu.VMEM((ns, 1, W), F32),
                pltpu.VMEM((PAIRS, keys, half), F32),
                pltpu.VMEM((PAIRS, keys, 2 * half), F32),
                pltpu.VMEM((PAIRS, ny, nx, 2, block, half), F32),
                pltpu.VMEM((PAIRS, ny, nx, block, half), F32),
                pltpu.VMEM((PAIRS, nx, ny, block, half), F32),
                pltpu.VMEM((PAIRS, nx, ny, block, half), F32),
                pltpu.VMEM((PAIRS, ny, block, half), F32),
                pltpu.VMEM((PAIRS, ny, block, half), F32),
                pltpu.VMEM((nz, res, W), F32),
                pltpu.VMEM((nz, res, W), F32),
                pltpu.VMEM((ns, chunk, 2 * W), F32),
                pltpu.VMEM((ns, chunk, 2 * W), F32),
                pltpu.VMEM((ns, chunk, 3 * W), F32),
                pltpu.VMEM((ns, chunk, 3 * W), F32),
                pltpu.VMEM((chunk, 5 * W), F32),
                pltpu.VMEM((nz, chunk, 5 * W), F32),
                pltpu.VMEM((ns, chunk, 5 * W), F32),
                pltpu.SemaphoreType.DMA((9,)),
                pltpu.SemaphoreType.DMA((9,)),
                pltpu.SemaphoreType.DMA((3, PAIRS)),
                pltpu.SemaphoreType.DMA((3, PAIRS)),
            ],
            compiler_params=pltpu.CompilerParams(
                collective_id=0, has_side_effects=True, vmem_limit_bytes=48 * 1024 * 1024
            ),
        )(
            alignment,
            cotangent,
            pair_bias,
            norm_gains,
            row_project,
            row_output,
            column_project,
            column_output,
            rmask,
            smask,
        )

    placed = (
        P("seq", "res", None),
        P("seq", "res", None),
        P(None, "res", None),
        P(),
        P(),
        P(),
        P(),
        P(),
        P("res"),
        P("seq"),
    )
    return jax.shard_map(
        local,
        mesh=mesh,
        in_specs=placed,
        out_specs=(P("seq", "res", None), P(None, "res", "seq"), P(), P(), P(), P(), P()),
        check_vma=False,
    )
```

time: 1730 us -> 89.2 us (0.05)
  blocking collectives: 1040 us -> 0 us
  waiting for transfers between devices: 587 us -> 0 us
  Pallas kernels: 0 us -> 75.8 us
  matrix products: 37.3 us -> 0 us
  local copies, waits for them, and re-layouts: 36.2 us -> 12.2 us
    psum x3 -> x0, blocking collectives: 750 us -> none  [the longest x2 504 us: local(): lax.psum((local_sum, jnp.sum(present), gated_local), 'seq')]
    psum x2 -> x0, waiting for transfers between devices: 524 us -> none  [local(): lax.psum((jnp.stack([grad_gain_row, grad_gain_col]), grad_row_project, gr...]
    pmax x1 -> x0, blocking collectives: 246 us -> none  [local(): peak_col = lax.pmax(jnp.max(scores_col, axis=0), 'seq')]
    pallas_call x0 -> x1, Pallas kernels: none -> 75.8 us  [local(): pl.pallas_call(functools.partial(kernel, (ny, nx, nz)), out_shape=(jax.Sh...]
    unnamed x5 -> x0, waiting for transfers between devices: 63.4 us -> none
    dot_general x43 -> x0, matrix products: 37.3 us -> none  [the longest x4 4.67 us: row_softmax(): jnp.einsum('qhd,khd->hqk', queries, key_rows, precision=PRECISE)]
    unnamed x1 -> x0, blocking collectives: 20.2 us -> none
    all_gather x1 -> x0, blocking collectives: 19.4 us -> none  [local(): lax.all_gather(memory_local, 'res', axis=1, tiled=True)]
  transfers between devices with their start and end apart: 4 -> 0, of which waited for: 3 -> 0; matrix products, arithmetic and copies ran while one was open for 1% -> 0% of each run, Pallas kernels for 0% -> 0%
where the time goes in v1:
time: 89.2 us; the launch traced here: 88.6 us
  Pallas kernels  75.8 us (85%)
  local copies, waits for them, and re-layouts  12.2 us (14%)
    pallas_call x1, Pallas kernels, local(): pl.pallas_call(functools.partial(kernel, (ny, nx, nz)), out_shape=(jax.Sh...  75.8 us
    unnamed x26, local copies, waits for them, and re-layouts  11.3 us

profile of v1, /device:TPU:1, one launch (start us, length us, event | category | flops | bytes accessed | tf_op | source)
XLA Modules:
  0.0 88.6 jit_solution(6732412619414256312)
XLA Ops:
  0.6 0.0 copy-start.8
  0.6 0.6 copy-done.8
  1.3 0.0 copy-start.9
  1.3 0.6 copy-done.9
  1.9 0.1 broadcast_in_dim.7
  2.0 0.0 copy-start.7
  2.0 0.1 broadcast_in_dim_reshape.3.smask_ref
  2.1 0.6 copy-done.7
  2.7 0.0 copy-start
  2.7 1.0 %copy-done = bf16[8,64,512]{2,1,0:T(8,128)(2,1)S(1)} copy-done((bf16[8,64,512]{2,1,0:T(8,128)(2,1)S(1)}, bf16[8,64,512]{2,1,0:T(8,128)(2,1)}, u32[]{:S(2)}) %copy-start) | copy-done | bytes 524312
  3.7 0.0 copy-start.1
  3.7 0.8 copy-done.1
  4.6 0.0 copy-start.2
  4.6 0.8 copy-done.2
  5.4 0.0 copy-start.3
  5.4 0.8 copy-done.3
  6.2 0.0 copy-start.4
  6.2 0.8 copy-done.4
  6.9 0.0 copy-start.5
  6.9 0.8 copy-done.5
  7.7 0.0 copy-start.6
  7.7 0.8 copy-done.6
  8.4 75.8 %shard_map.153 = (bf16[2,64,64]{2,1,0:T(8,128)(2,1)S(1)}, f32[8,64,8]{2,1,0:T(8,128)S(1)}, f32[2,64]{1,0:T(2,128)S(1)}, f32[64,256]{1,0:T(8,128)S(1)}, f32[64,64...) custom-call(bf16[2,64,64]{2,1,0:T(8,128)(2,1)S(1)} %copy-done.3, bf16[2,64,64]{2,1,0:T(8,128)(2,1)S(1)} %copy-done.4, ...), custom_call_target="tpu_custom_call" | custom-call | tf_op jit(solution)/shard_map/pallas_call | solution.py:609
  84.2 0.7 copy.17
  85.0 0.6 copy.24
  85.6 0.6 copy.25
  86.2 0.6 copy.26
  86.8 0.6 copy.27
  87.4 0.6 copy.28
  88.0 0.6 copy.29
  (1 shorter events, 0.0 us)
Async XLA Ops:
  0.6 0.7 copy-start.8
  1.3 0.7 copy-start.9
  2.0 0.7 copy-start.7
  2.7 1.0 %copy-start = (bf16[8,64,512]{2,1,0:T(8,128)(2,1)S(1)}, bf16[8,64,512]{2,1,0:T(8,128)(2,1)}, u32[]{:S(2)}) copy-start(bf16[8,64,512]{2,1,0:T(8,128)(2,1)} %bias_ref.1) | copy-start | bytes 1572868
  3.7 0.8 copy-start.1
  4.6 0.8 copy-start.2
  5.4 0.8 copy-start.3
  6.2 0.8 copy-start.4
  6.9 0.8 copy-start.5
  7.7 0.8 copy-start.6

commit v2 on v1

--- a/solution.py
+++ b/solution.py
@@ -79,16 +79,16 @@
 
 def kernel(
     sizes,
-    align_ref,
-    cot_ref,
-    bias_ref,
-    gains_ref,
-    rowp_ref,
-    rowo_ref,
-    colp_ref,
-    colo_ref,
-    rmask_ref,
-    smask_ref,
+    align_hbm,
+    cot_hbm,
+    bias_hbm,
+    gains_hbm,
+    rowp_hbm,
+    rowo_hbm,
+    colp_hbm,
+    colo_hbm,
+    rmask_hbm,
+    smask_hbm,
     galign_ref,
     gbias_ref,
     ggains_ref,
@@ -120,10 +120,23 @@
     t_s,
     t_r,
     o_r,
+    align_ref,
+    cot_ref,
+    bias_ref,
+    gains_ref,
+    rowp_ref,
+    rowo_ref,
+    colp_ref,
+    colo_ref,
+    rmask_ref,
+    smask_ref,
     send_sem,
     recv_sem,
     bias_send,
     bias_recv,
+    load_sem,
+    gather_send,
+    gather_recv,
 ):
     ny, nx, nz = sizes
     ns = ny * nx * 2
@@ -139,6 +152,37 @@
     my = me // (2 * nx)
     scaling = DH ** (-0.5)
 
+    sources = (
+        align_hbm,
+        rmask_hbm,
+        smask_hbm,
+        cot_hbm,
+        gains_hbm,
+        rowp_hbm,
+        rowo_hbm,
+        bias_hbm,
+        colp_hbm,
+        colo_hbm,
+    )
+    targets = (
+        align_ref,
+        rmask_ref,
+        smask_ref,
+        cot_ref,
+        gains_ref,
+        rowp_ref,
+        rowo_ref,
+        bias_ref,
+        colp_ref,
+        colo_ref,
+    )
+    loads = [
+        pltpu.make_async_copy(source, target, load_sem.at[i])
+        for i, (source, target) in enumerate(zip(sources, targets))
+    ]
+    for load in loads:
+        load.start()
+
     barrier = pltpu.get_barrier_semaphore()
 
     def greet_seq(i, carry):
@@ -169,7 +213,8 @@
             ).start()
             return carry
 
-        lax.fori_loop(1, ns, one, 0)
+        lax.fori_loop(ns // 4, ns, one, 0)
+        lax.fori_loop(1, ns // 4, one, 0)
 
     def to_res(source, target, which):
         def one(i, carry):
@@ -197,13 +242,69 @@
     def keep(source, target, at):
         target[pl.ds(at, 1)] = source[pl.ds(at, 1)]
 
+    ring = (3, nz - 3, 2, nz - 2, 1, nz - 1)
+    cut = (res + 8) // 16 * 8
+
+    def gather_copy(step):
+        return pltpu.make_async_remote_copy(
+            src_ref=xall.at[mz],
+            dst_ref=xall.at[mz],
+            send_sem=gather_send.at[step],
+            recv_sem=gather_recv.at[step],
+            device_id=(me, lax.rem(mz + step, nz)),
+            device_id_type=MESH,
+        )
+
+    def gather_relay(step, rows, semaphore):
+        part = xall.at[lax.rem(mz + nz - step, nz), rows]
+        return pltpu.make_async_remote_copy(
+            src_ref=part,
+            dst_ref=part,
+            send_sem=gather_send.at[semaphore],
+            recv_sem=gather_recv.at[semaphore],
+            device_id=(me, lax.rem(mz + (nz // 2 - step) + nz, nz)),
+            device_id_type=MESH,
+        )
+
+    relays = ((3, pl.ds(0, cut), 0), (nz - 3, pl.ds(cut, res + 8 - cut), 4))
+
+    def gather_start():
+        if nz != 8:
+            to_res(lambda j: xall.at[mz], xall, 0)
+            return
+        for step in ring:
+            gather_copy(step).start()
+
+    def gather_pass_on():
+        if nz != 8:
+            return
+        for step, rows, semaphore in relays:
+            gather_copy(step).wait_recv()
+            gather_relay(step, rows, semaphore).start()
+
+    def gather_wait():
+        if nz != 8:
+            wait_all(xall, 0, nz)
+            return
+        for step in ring[2:]:
+            gather_copy(step).wait_recv()
+        for relay in relays:
+            gather_relay(*relay).wait_recv()
+
+    def gather_finish():
+        if nz != 8:
+            return
+        for step in ring:
+            gather_copy(step).wait_send()
+        for relay in relays:
+            gather_relay(*relay).wait_send()
+
+    for load in loads[:4]:
+        load.wait()
     align = align_ref[...].astype(F32)
     initial = jnp.concatenate([align[0], align[1]], axis=1)
     cot = cot_ref[...].astype(F32)
     top_local = jnp.concatenate([cot[0], cot[1]], axis=1)
-    gains = gains_ref[...]
-    gain_row = twice(gains[0:1])
-    gain_col = twice(gains[1:2])
     averaging = ones_where(iota((W, W), 0) // C == iota((W, W), 1) // C) * (1.0 / C)
 
     def layer_norm(values):
@@ -220,15 +321,26 @@
 
     hat_local, inverse_local = layer_norm(initial)
     xall[mz, 0:res, :] = hat_local
-    xall[mz, res : res + 8, :] = jnp.broadcast_to(rmask_ref[...].astype(F32), (8, W))
-    present_row = smask_ref[...].astype(F32)
+    xall[mz, res : res + 8, :] = jnp.broadcast_to(
+        jnp.concatenate([rmask_ref[...].astype(F32), jnp.zeros((1, W - res), F32)], axis=1), (8, W)
+    )
+    present_pair = smask_ref[...].astype(F32)
+    present_row = jnp.concatenate(
+        [jnp.broadcast_to(present_pair[:, i : i + 1], (1, C)) for i in range(L)], axis=1
+    )
     gsend[:, 0, 0:W] = top_local
     gsend[:, 0, W : 2 * W] = jnp.broadcast_to(present_row, (res, W))
 
     pl.semaphore_wait(barrier, ns + nz - 2)
-    to_res(lambda j: xall.at[mz], xall, 0)
+    gather_start()
     to_seq(lambda j: gsend.at[j], grecv, 1)
     keep(gsend, grecv, me)
+
+    for load in loads[4:]:
+        load.wait()
+    gains = gains_ref[...]
+    gain_row = twice(gains[0:1])
+    gain_col = twice(gains[1:2])
 
     lane = iota((C, W), 1)
     column = (lane // 32) * 16 + lane % 16
@@ -255,6 +367,7 @@
     queries = dot(normed_local, query_w) * scaling
     gate_row = jax.nn.sigmoid(dot(normed_local, gate_w))
 
+    gather_pass_on()
     for p in range(PAIRS):
         pair = bias_ref[2 * p : 2 * p + 2].astype(F32).reshape(half, keys)
         bias_t[p] = pair.T
@@ -285,6 +398,7 @@
         both = kept[:, :half] + kept[:, half:]
         return both[:, :res] + both[:, res:]
 
+    identity = ones_where(iota((C, C), 0) == iota((C, C), 1))
     colp = colp_ref[...]
     colo = colo_ref[...]
     entry = iota((C + 2 * DH + C, C), 0)
@@ -297,7 +411,7 @@
     column_w = jnp.concatenate([key_col_w, value_col_w, gate_col_w], axis=1)
     head_sum = ones_where(iota((W, W), 0) // DH == iota((W, W), 1) // DH)
 
-    wait_all(xall, 0, nz)
+    gather_wait()
     hat_all = xall[:, 0:res, :].reshape(keys, W)
     normed_all = hat_all * gain_row
     memory = dot(normed_all, memory_w)
@@ -378,9 +492,9 @@
 
     pack_lane = iota((C, 2 * W), 1)
     pack_row = iota((C, 2 * W), 0)
-    grad_full = dot(normed_col, grad_projected, TN)
-    identity = ones_where(iota((C, C), 0) == iota((C, C), 1))
-    mean_column = jnp.sum(identity * mean_normed[:, :C], axis=1, keepdims=True)
+    grad_full = dot(hat_col, grad_projected, TN)
+    mean_hat = fold(jnp.sum(present * hat_col, axis=0, keepdims=True)) * inverse_count
+    mean_column = jnp.sum(identity * mean_hat[:, :C], axis=1, keepdims=True)
     grad_col_parts = jnp.concatenate(
         [
             mean_column * grad_query_col[:, :C],
@@ -401,11 +515,7 @@
         ],
         axis=0,
     )
-    gain_sums = fold(jnp.sum(grad_normed_col * hat_col, axis=0, keepdims=True))
-    gain_column = jnp.sum(identity * gain_sums[:, :C], axis=1, keepdims=True)
-    pack = dot(grad_col_parts, placing) + jnp.where(
-        pack_lane == 3 * C + 2 * DH, gain_column, 0.0
-    )
+    pack = dot(grad_col_parts, placing)
     pc_s[...] = pack.reshape(ns, C // ns, 2 * W)
     to_seq(lambda j: pc_s.at[j], pc_r, 4)
     keep(pc_s, pc_r, me)
@@ -420,6 +530,8 @@
     grad_gated = dot(grad_middle, out_w, NT)
     grad_gate = grad_gated * mixture * gate_row * (1.0 - gate_row)
     grads_apart = heads_apart(grad_gated * gate_row)
+    grad_out_w = dot(gated, grad_middle, TN)
+    grad_rowo = dot(chosen[0], grad_out_w[:, :C]) + dot(chosen[1], grad_out_w[:, C:])
 
     def bias_core(p):
         return pltpu.make_async_remote_copy(
@@ -476,9 +588,8 @@
         wait(part, bias_recv.at[2, p])
         wait(part, bias_send.at[2, p])
         total = sum([y_r[p, i] for i in range(1, ny)], y_r[p, 0])
-        flat = total.T
-        gbias_ref[2 * p] = flat[:res]
-        gbias_ref[2 * p + 1] = flat[res:]
+        gbias_ref[2 * p] = total[:, :res]
+        gbias_ref[2 * p + 1] = total[:, res:]
 
     grad_keys = jnp.zeros((keys, W), F32)
     grad_values = jnp.zeros((keys, W), F32)
@@ -505,29 +616,12 @@
         )
         if p >= 1:
             bias_to_x(p - 1)
-        if p >= 2:
-            bias_to_y(p - 2)
 
     grad_memory = jnp.concatenate([grad_keys, grad_values], axis=1)
-    partial = dot3(grad_memory, memory_w, NT)
-    zr_s[...] = partial.reshape(nz, res, W)
-    to_res(lambda j: zr_s.at[j], zr_r, 5)
-    keep(zr_s, zr_r, mz)
-    bias_to_x(PAIRS - 1)
-
     grad_query = jnp.concatenate(grad_queries, axis=0).T * scaling
     own_grads = jnp.concatenate([grad_query, grad_gate], axis=1)
-    own_weights = jnp.concatenate([query_w, gate_w], axis=1)
-    own_normed_grad = dot(own_grads, own_weights, NT)
-    grad_memory_w = dot3(normed_all, grad_memory, TN)
-    grad_own_w = dot(normed_local, own_grads, TN)
-    grad_out_w = dot(gated, grad_middle, TN)
-    gain_sums_row = fold(
-        jnp.sum(partial * hat_all, axis=0, keepdims=True)
-        + jnp.sum(own_normed_grad * hat_local, axis=0, keepdims=True)
-    )
-    gain_column_row = jnp.sum(identity * gain_sums_row[:, :C], axis=1, keepdims=True)
-    grad_rowo = dot(chosen[0], grad_out_w[:, :C]) + dot(chosen[1], grad_out_w[:, C:])
+    grad_memory_w = dot3(hat_all, grad_memory, TN)
+    grad_own_w = dot(hat_local, own_grads, TN)
     pack_row_part = jnp.concatenate(
         [
             gather_columns(grad_own_w[:, :W]),
@@ -535,14 +629,21 @@
             gather_columns(grad_memory_w[:, W:]),
             gather_columns(grad_own_w[:, W:]),
             grad_rowo,
-            jnp.broadcast_to(gain_column_row, (C, C)),
+            jnp.zeros((C, C), F32),
         ],
         axis=1,
     )
     pr_s[...] = pack_row_part.reshape(ns, C // ns, 3 * W)
     to_seq(lambda j: pr_s.at[j], pr_r, 6)
     keep(pr_s, pr_r, me)
-    bias_to_y(PAIRS - 2)
+
+    zr_s[...] = dot3(grad_memory, memory_w, NT).reshape(nz, res, W)
+    to_res(lambda j: zr_s.at[j], zr_r, 5)
+    keep(zr_s, zr_r, mz)
+    bias_to_x(PAIRS - 1)
+    own_normed_grad = dot(own_grads, jnp.concatenate([query_w, gate_w], axis=1), NT)
+    for p in range(PAIRS):
+        bias_to_y(p)
 
     wait_all(pc_r, 4, ns)
     wait_all(pr_r, 6, ns)
@@ -551,7 +652,6 @@
     )
     to_res(lambda j: t_s, t_r, 7)
     t_r[pl.ds(mz, 1)] = t_s[...][None]
-    bias_to_y(PAIRS - 1)
 
     wait_all(zr_r, 5, nz)
     grad_normed_row = sum([zr_r[i] for i in range(1, nz)], zr_r[0]) + own_normed_grad
@@ -565,17 +665,44 @@
     to_seq(lambda j: o_r.at[me], o_r, 8)
     for p in range(PAIRS):
         bias_done(p)
+    gather_finish()
+    gain_columns = [
+        jnp.sum(identity * gains[i : i + 1], axis=1, keepdims=True) for i in range(2)
+    ]
     wait_all(o_r, 8, ns)
     final = o_r[...].reshape(C, 5 * W)
-    growp_ref[...] = final[:, 0 : 4 * C]
+    row_part = final[:, 0 : 4 * C]
+    col_part = final[:, 3 * W : 3 * W + 2 * C + 2 * DH]
+    growp_ref[...] = row_part * gain_columns[0]
     growo_ref[...] = final[:, 4 * C : 5 * C]
-    column_part = final[:, 3 * W :]
-    gcolp_ref[...] = column_part[:, 0 : 2 * C + 2 * DH]
-    gcolo_ref[...] = column_part[:, 2 * C + 2 * DH : 3 * C + 2 * DH]
-    row_gain = final[:, 2 * W : 3 * W].T[C : C + 1]
-    col_gain = column_part[:, W:].T[3 * C + 2 * DH - W : 3 * C + 2 * DH - W + 1]
-    ggains_ref[0:1, :] = row_gain
-    ggains_ref[1:2, :] = col_gain
+    gcolp_ref[...] = col_part * gain_columns[1]
+    gcolo_ref[...] = final[:, 3 * W + 2 * C + 2 * DH : 3 * W + 3 * C + 2 * DH]
+    for i, (part, weights) in enumerate(((row_part, rowp), (col_part, colp))):
+        column_sum = jnp.sum(part * weights, axis=1, keepdims=True)
+        ggains_ref[i : i + 1, :] = jnp.sum(identity * column_sum, axis=0, keepdims=True)
+
+
+def store_all(*refs):
+    count = (len(refs) - 1) // 2
+    semaphores = refs[-1]
+    copies = [
+        pltpu.make_async_copy(refs[i], refs[count + i], semaphores.at[i]) for i in range(count)
+    ]
+    for copy in copies:
+        copy.start()
+    for copy in copies:
+        copy.wait()
+
+
+def finish(arrays):
+    arrays = pl.pallas_call(
+        store_all,
+        out_shape=tuple(jax.ShapeDtypeStruct(a.shape, a.dtype) for a in arrays),
+        in_specs=[pl.BlockSpec(memory_space=pltpu.VMEM)] * len(arrays),
+        out_specs=(pl.BlockSpec(memory_space=pltpu.HBM),) * len(arrays),
+        scratch_shapes=[pltpu.SemaphoreType.DMA((len(arrays),))],
+    )(*arrays)
+    return (arrays[0], jnp.swapaxes(arrays[1], 1, 2)) + tuple(arrays[2:])
 
 
 def solution(mesh):
@@ -601,23 +728,21 @@
         residue_mask,
         sequence_mask,
     ):
-        rmask = jnp.pad(residue_mask[None], ((0, 0), (0, W - res)))
-        smask = jnp.repeat(sequence_mask, C)[None]
         vmem = pl.BlockSpec(memory_space=pltpu.VMEM)
         ns = seq_devices
         chunk = C // ns
-        return pl.pallas_call(
+        outs = pl.pallas_call(
             functools.partial(kernel, (ny, nx, nz)),
             out_shape=(
                 jax.ShapeDtypeStruct((L, res, C), BF16),
-                jax.ShapeDtypeStruct((H, res, block), F32),
+                jax.ShapeDtypeStruct((H, block, res), F32),
                 jax.ShapeDtypeStruct((2, C), F32),
                 jax.ShapeDtypeStruct((C, 4 * C), F32),
                 jax.ShapeDtypeStruct((C, C), F32),
                 jax.ShapeDtypeStruct((C, 2 * C + 2 * DH), F32),
                 jax.ShapeDtypeStruct((C, C), F32),
             ),
-            in_specs=[vmem] * 10,
+            in_specs=[pl.BlockSpec(memory_space=pltpu.HBM)] * 10,
             out_specs=(vmem,) * 7,
             scratch_shapes=[
                 pltpu.VMEM((nz, res + 8, W), F32),
@@ -644,13 +769,26 @@
                 pltpu.VMEM((chunk, 5 * W), F32),
                 pltpu.VMEM((nz, chunk, 5 * W), F32),
                 pltpu.VMEM((ns, chunk, 5 * W), F32),
+                pltpu.VMEM((L, res, C), BF16),
+                pltpu.VMEM((L, res, C), BF16),
+                pltpu.VMEM((H, res, keys), BF16),
+                pltpu.VMEM((2, C), F32),
+                pltpu.VMEM((C, 4 * C), F32),
+                pltpu.VMEM((C, C), F32),
+                pltpu.VMEM((C, 2 * C + 2 * DH), F32),
+                pltpu.VMEM((C, C), F32),
+                pltpu.VMEM((1, res), jnp.int32),
+                pltpu.VMEM((1, L), jnp.int32),
                 pltpu.SemaphoreType.DMA((9,)),
                 pltpu.SemaphoreType.DMA((9,)),
                 pltpu.SemaphoreType.DMA((3, PAIRS)),
                 pltpu.SemaphoreType.DMA((3, PAIRS)),
+                pltpu.SemaphoreType.DMA((10,)),
+                pltpu.SemaphoreType.DMA((8,)),
+                pltpu.SemaphoreType.DMA((8,)),
             ],
             compiler_params=pltpu.CompilerParams(
-                collective_id=0, has_side_effects=True, vmem_limit_bytes=48 * 1024 * 1024
+                collective_id=0, has_side_effects=True, vmem_limit_bytes=64 * 1024 * 1024
             ),
         )(
             alignment,
@@ -661,9 +799,10 @@
             row_output,
             column_project,
             column_output,
-            rmask,
-            smask,
+            residue_mask[None],
+            sequence_mask[None],
         )
+        return finish(outs)
 
     placed = (
         P("seq", "res", None),

time: 89.2 us -> 72.4 us (0.81)
  local copies, waits for them, and re-layouts: 12.2 us -> 0 us
  Pallas kernels: 75.8 us -> 71.6 us
    unnamed x26 -> x0, local copies, waits for them, and re-layouts: 11.3 us -> none
    pallas_call x1, Pallas kernels: 75.8 us -> 69.9 us  [local(): pl.pallas_call(functools.partial(kernel, (ny, nx, nz)), out_shape=(jax.Sh...]
    pallas_call x0 -> x1, Pallas kernels: none -> 1.65 us  [finish(): pl.pallas_call(store_all, out_shape=tuple((jax.ShapeDtypeStruct(a.shape,...]
where the time goes in v2:
time: 72.4 us; the launch traced here: 72.2 us
  Pallas kernels  71.6 us (99%)
    pallas_call x1, Pallas kernels, local(): pl.pallas_call(functools.partial(kernel, (ny, nx, nz)), out_shape=(jax.Sh...  69.9 us
    pallas_call x1, Pallas kernels, finish(): pl.pallas_call(store_all, out_shape=tuple((jax.ShapeDtypeStruct(a.shape,...  1.65 us

profile of v2, /device:TPU:1, one launch (start us, length us, event | category | flops | bytes accessed | tf_op | source)
XLA Modules:
  0.0 72.2 jit_solution(14291751217364404075)
XLA Ops:
  0.6 69.9 %shard_map.153 = (bf16[2,64,64]{2,1,0:T(8,128)(2,1)}, f32[8,8,64]{2,1,0:T(8,128)}, f32[2,64]{1,0:T(2,128)}, f32[64,256]{1,0:T(8,128)}, f32[64,64]{1,0:T(8,128)}, /*index=5*/f32[64,144]{1,0:T(8,128)}, f32[64,64]{1,0:T(8,128)}) custom-call(bf16[2,64,64]{2,1,0:T(8,128)(2,1)} %align_hbm.1, bf16[2,64,64]{2,1,0:T(8,128)(2,1)} %cot_hbm.1, ...), custom_call_target="tpu_custom_call" | custom-call | tf_op jit(solution)/shard_map/pallas_call | solution.py:734
  70.5 1.6 %shard_map.154 = (bf16[2,64,64]{2,1,0:T(8,128)(2,1)}, f32[8,8,64]{2,1,0:T(8,128)}, f32[2,64]{1,0:T(2,128)}, f32[64,256]{1,0:T(8,128)}, f32[64,64]{1,0:T(8,128)}, /*index=5*/f32[64,144]{1,0:T(8,128)}, f32[64,64]{1,0:T(8,128)}) custom-call(bf16[2,64,64]{2,1,0:T(8,128)(2,1)} %get-tuple-element.21.refs_0_, f32[8,8,64]{2,1,0:T(8,128)} %get-tuple-element.22.refs_1_, ...), custom_call_target="tpu_custom_call" | custom-call | tf_op jit(solution)/shard_map/pallas_call | solution.py:698

commit v3 on v2

--- a/solution.py
+++ b/solution.py
@@ -50,6 +50,32 @@
     return dot1(ah, bh, dims) + (dot1(ah, bl, dims) + dot1(al, bh, dims))
 
 
+def products(first, second):
+    a1, a2, a3 = first
+    b1, b2, b3 = second
+    a12 = jnp.concatenate([a1, a2], axis=1)
+    a13 = jnp.concatenate([a1, a3], axis=1)
+    return dot1(a12, jnp.concatenate([b1, b1], axis=0)) + (
+        dot1(a12, jnp.concatenate([b2, b2], axis=0)) + dot1(a13, jnp.concatenate([b3, b1], axis=0))
+    )
+
+
+def pick(values, ones, dims=NN):
+    ones = ones.astype(BF16)
+    axis = dims[0][1][0]
+    return dot1(
+        jnp.concatenate(split2(values), axis=1), jnp.concatenate([ones, ones], axis=axis), dims
+    )
+
+
+def outer3(left, right):
+    lh, ll = left
+    rh, rl = right
+    both = dot1(lh, jnp.concatenate([rh, rl], axis=0), NT)
+    count = rh.shape[0]
+    return both[:, :count] + (both[:, count:] + dot1(ll, rh, NT))
+
+
 def iota(shape, axis):
     return lax.broadcasted_iota(jnp.int32, shape, axis)
 
@@ -89,13 +115,13 @@
     colo_hbm,
     rmask_hbm,
     smask_hbm,
-    galign_ref,
-    gbias_ref,
-    ggains_ref,
-    growp_ref,
-    growo_ref,
-    gcolp_ref,
-    gcolo_ref,
+    galign_hbm,
+    gbias_hbm,
+    ggains_hbm,
+    growp_hbm,
+    growo_hbm,
+    gcolp_hbm,
+    gcolo_hbm,
     xall,
     gsend,
     grecv,
@@ -120,6 +146,9 @@
     t_s,
     t_r,
     o_r,
+    tc_s,
+    tc_r,
+    oc_r,
     align_ref,
     cot_ref,
     bias_ref,
@@ -137,6 +166,14 @@
     load_sem,
     gather_send,
     gather_recv,
+    galign_ref,
+    gbias_ref,
+    ggains_ref,
+    growp_ref,
+    growo_ref,
+    gcolp_ref,
+    gcolo_ref,
+    store_sem,
 ):
     ny, nx, nz = sizes
     ns = ny * nx * 2
@@ -198,7 +235,23 @@
         return carry
 
     lax.fori_loop(1, nz, greet_res, 0)
-    lax.fori_loop(1, ns, greet_seq, 0)
+    lax.fori_loop(ns // 4, ns, greet_seq, 0)
+    lax.fori_loop(1, ns // 4, greet_seq, 0)
+
+    stores = [
+        pltpu.make_async_copy(source, target, store_sem.at[i])
+        for i, (source, target) in enumerate(
+            (
+                (galign_ref, galign_hbm),
+                (gbias_ref, gbias_hbm),
+                (ggains_ref, ggains_hbm),
+                (growp_ref, growp_hbm),
+                (growo_ref, growo_hbm),
+                (gcolp_ref, gcolp_hbm),
+                (gcolo_ref, gcolo_hbm),
+            )
+        )
+    ]
 
     def to_seq(source, target, which):
         def one(i, carry):
@@ -351,9 +404,6 @@
     def spread_columns(weights):
         return jnp.concatenate([dot(weights, chosen[0]), dot(weights, chosen[1])], axis=0)
 
-    def gather_columns(full):
-        return dot(full[:C], chosen[0], NT) + dot(full[C:], chosen[1], NT)
-
     rowp = rowp_ref[...]
     query_w = spread_columns(rowp[:, 0:C])
     key_w = spread_columns(rowp[:, C : 2 * C])
@@ -380,16 +430,7 @@
         return [jnp.where(match == 4 * p, flat, 0.0) for p in range(PAIRS)]
 
     queries_apart = heads_apart(queries)
-    query_terms = []
-    for p in range(PAIRS):
-        q1, q2, q3 = split3(queries_apart[p])
-        query_terms.append(
-            (
-                jnp.concatenate([q1, q1], axis=0),
-                jnp.concatenate([q2, q2], axis=0),
-                jnp.concatenate([q3, q1], axis=0),
-            )
-        )
+    query_terms = [split3(apart) for apart in queries_apart]
 
     mine = ones_where(iota((32, wide), 0) // DH == iota((32, wide), 1) // res)
 
@@ -414,7 +455,7 @@
     gather_wait()
     hat_all = xall[:, 0:res, :].reshape(keys, W)
     normed_all = hat_all * gain_row
-    memory = dot(normed_all, memory_w)
+    memory = products(split3(normed_all), split3(memory_w))
     key_rows = memory[:, :W]
     value_rows = memory[:, W:]
     value_flat = value_rows.T
@@ -422,16 +463,13 @@
     key_bias = jnp.concatenate(
         [MASKED * (mask_flat[:res, 8 * z : 8 * z + 1] - 1.0) for z in range(nz)], axis=0
     )
-    k1, k2, k3 = split3(key_rows)
-    k12 = jnp.concatenate([k1, k2], axis=1)
-    k13 = jnp.concatenate([k1, k3], axis=1)
+    key_terms = split3(key_rows)
     value_high, value_low = split2(value_flat)
 
     totals = []
     mixed = []
     for p in range(PAIRS):
-        terms = query_terms[p]
-        scores = dot1(k12, terms[0]) + (dot1(k12, terms[1]) + dot1(k13, terms[2]))
+        scores = products(key_terms, query_terms[p])
         scores = scores + twice(bias_t[p]) + key_bias
         peak = jnp.max(scores, axis=0, keepdims=True)
         exponent = jnp.exp(scores - peak)
@@ -449,6 +487,12 @@
     msend[:, 0, :] = middle
     to_seq(lambda j: msend.at[j], mrecv, 2)
     keep(msend, mrecv, me)
+
+    key_flat = key_rows.T
+    key_high, key_low = split2(key_flat)
+    v1, v2 = split2(value_rows)
+    hat_high, hat_low = split2(hat_all.T)
+    v12 = jnp.concatenate([v1, v2], axis=1)
 
     wait_all(grecv, 1, ns)
     top = grecv[:, 0, 0:W]
@@ -515,22 +559,17 @@
         ],
         axis=0,
     )
-    pack = dot(grad_col_parts, placing)
+    pack = pick(grad_col_parts, placing)
     pc_s[...] = pack.reshape(ns, C // ns, 2 * W)
     to_seq(lambda j: pc_s.at[j], pc_r, 4)
     keep(pc_s, pc_r, me)
-
-    key_flat = key_rows.T
-    key_high, key_low = split2(key_flat)
-    v1, v2 = split2(value_rows)
-    v12 = jnp.concatenate([v1, v2], axis=1)
 
     wait_all(brecv, 3, ns)
     grad_middle = brecv[:, 0, :]
     grad_gated = dot(grad_middle, out_w, NT)
     grad_gate = grad_gated * mixture * gate_row * (1.0 - gate_row)
     grads_apart = heads_apart(grad_gated * gate_row)
-    grad_out_w = dot(gated, grad_middle, TN)
+    grad_out_w = dot3(gated, grad_middle, TN)
     grad_rowo = dot(chosen[0], grad_out_w[:, :C]) + dot(chosen[1], grad_out_w[:, C:])
 
     def bias_core(p):
@@ -606,52 +645,61 @@
         bias_core(p).start()
         sh, sl = split2(grad_scores)
         wh, wl = split2(weights)
-        q1, q2 = split2(queries_apart[p])
-        grad_keys = grad_keys + (dot1(sh, q1, NT) + (dot1(sh, q2, NT) + dot1(sl, q1, NT)))
-        grad_values = grad_values + (dot1(wh, gh, NT) + (dot1(wh, gl, NT) + dot1(wl, gh, NT)))
+        grad_keys = grad_keys + outer3((sh, sl), query_terms[p][:2])
+        grad_values = grad_values + outer3((wh, wl), (gh, gl))
         kh = key_high[32 * p : 32 * p + 32]
         kl = key_low[32 * p : 32 * p + 32]
         grad_queries.append(
             heads_together(dot1(kh, sh) + (dot1(kl, sh) + dot1(kh, sl)))
         )
-        if p >= 1:
-            bias_to_x(p - 1)
 
     grad_memory = jnp.concatenate([grad_keys, grad_values], axis=1)
     grad_query = jnp.concatenate(grad_queries, axis=0).T * scaling
     own_grads = jnp.concatenate([grad_query, grad_gate], axis=1)
-    grad_memory_w = dot3(hat_all, grad_memory, TN)
-    grad_own_w = dot(hat_local, own_grads, TN)
+    gh, gl = split2(grad_memory)
+    grad_memory_w = dot1(hat_high, gh) + (dot1(hat_high, gl) + dot1(hat_low, gh))
+    grad_own_w = dot3(hat_local, own_grads, TN)
+    grad_parts = (
+        grad_own_w[:, :W],
+        grad_memory_w[:, :W],
+        grad_memory_w[:, W:],
+        grad_own_w[:, W:],
+    )
+    gathered = pick(
+        jnp.concatenate([part[:C] for part in grad_parts], axis=0), chosen[0], NT
+    ) + pick(jnp.concatenate([part[C:] for part in grad_parts], axis=0), chosen[1], NT)
     pack_row_part = jnp.concatenate(
-        [
-            gather_columns(grad_own_w[:, :W]),
-            gather_columns(grad_memory_w[:, :W]),
-            gather_columns(grad_memory_w[:, W:]),
-            gather_columns(grad_own_w[:, W:]),
-            grad_rowo,
-            jnp.zeros((C, C), F32),
-        ],
+        [gathered[i * C : (i + 1) * C] for i in range(4)] + [grad_rowo, jnp.zeros((C, C), F32)],
         axis=1,
     )
     pr_s[...] = pack_row_part.reshape(ns, C // ns, 3 * W)
     to_seq(lambda j: pr_s.at[j], pr_r, 6)
     keep(pr_s, pr_r, me)
 
+    for p in range(PAIRS):
+        bias_to_x(p)
+    wait_all(pc_r, 4, ns)
+    tc_s[...] = jnp.sum(pc_r[...], axis=0)
+    to_res(lambda j: tc_s, tc_r, 9)
+    tc_r[pl.ds(mz, 1)] = tc_s[...][None]
+    own_normed_grad = dot(own_grads, jnp.concatenate([query_w, gate_w], axis=1), NT)
     zr_s[...] = dot3(grad_memory, memory_w, NT).reshape(nz, res, W)
+    keep(zr_s, zr_r, mz)
+    wait_all(tc_r, 9, nz)
+    oc_r[me] = sum([tc_r[i] for i in range(1, nz)], tc_r[0])
+    to_seq(lambda j: oc_r.at[me], oc_r, 10)
+
+    wait_all(pr_r, 6, ns)
+    t_s[...] = jnp.sum(pr_r[...], axis=0)
+    to_res(lambda j: t_s, t_r, 7)
+    t_r[pl.ds(mz, 1)] = t_s[...][None]
     to_res(lambda j: zr_s.at[j], zr_r, 5)
-    keep(zr_s, zr_r, mz)
-    bias_to_x(PAIRS - 1)
-    own_normed_grad = dot(own_grads, jnp.concatenate([query_w, gate_w], axis=1), NT)
     for p in range(PAIRS):
         bias_to_y(p)
 
-    wait_all(pc_r, 4, ns)
-    wait_all(pr_r, 6, ns)
-    t_s[...] = jnp.concatenate(
-        [jnp.sum(pr_r[...], axis=0), jnp.sum(pc_r[...], axis=0)], axis=1
-    )
-    to_res(lambda j: t_s, t_r, 7)
-    t_r[pl.ds(mz, 1)] = t_s[...][None]
+    wait_all(t_r, 7, nz)
+    o_r[me] = sum([t_r[i] for i in range(1, nz)], t_r[0])
+    to_seq(lambda j: o_r.at[me], o_r, 8)
 
     wait_all(zr_r, 5, nz)
     grad_normed_row = sum([zr_r[i] for i in range(1, nz)], zr_r[0]) + own_normed_grad
@@ -659,27 +707,39 @@
     grad_align = (grad_middle + grad_initial).astype(BF16)
     galign_ref[0] = grad_align[:, :C]
     galign_ref[1] = grad_align[:, C:]
-
-    wait_all(t_r, 7, nz)
-    o_r[me] = sum([t_r[i] for i in range(1, nz)], t_r[0])
-    to_seq(lambda j: o_r.at[me], o_r, 8)
+    stores[0].start()
     for p in range(PAIRS):
         bias_done(p)
+    stores[1].start()
     gather_finish()
     gain_columns = [
         jnp.sum(identity * gains[i : i + 1], axis=1, keepdims=True) for i in range(2)
     ]
+
+    def gain_gradient(part, weights):
+        column_sum = jnp.sum(part * weights, axis=1, keepdims=True)
+        return jnp.sum(identity * column_sum, axis=0, keepdims=True)
+
+    wait_all(oc_r, 10, ns)
+    final = oc_r[...].reshape(C, 2 * W)
+    part = final[:, 0 : 2 * C + 2 * DH]
+    gcolp_ref[...] = part * gain_columns[1]
+    gcolo_ref[...] = final[:, 2 * C + 2 * DH : 3 * C + 2 * DH]
+    ggains_ref[1:2, :] = gain_gradient(part, colp)
+    stores[5].start()
+    stores[6].start()
+
     wait_all(o_r, 8, ns)
-    final = o_r[...].reshape(C, 5 * W)
-    row_part = final[:, 0 : 4 * C]
-    col_part = final[:, 3 * W : 3 * W + 2 * C + 2 * DH]
-    growp_ref[...] = row_part * gain_columns[0]
+    final = o_r[...].reshape(C, 3 * W)
+    part = final[:, 0 : 4 * C]
+    growp_ref[...] = part * gain_columns[0]
     growo_ref[...] = final[:, 4 * C : 5 * C]
-    gcolp_ref[...] = col_part * gain_columns[1]
-    gcolo_ref[...] = final[:, 3 * W + 2 * C + 2 * DH : 3 * W + 3 * C + 2 * DH]
-    for i, (part, weights) in enumerate(((row_part, rowp), (col_part, colp))):
-        column_sum = jnp.sum(part * weights, axis=1, keepdims=True)
-        ggains_ref[i : i + 1, :] = jnp.sum(identity * column_sum, axis=0, keepdims=True)
+    stores[3].start()
+    stores[4].start()
+    ggains_ref[0:1, :] = gain_gradient(part, rowp)
+    stores[2].start()
+    for store in stores:
+        store.wait()
 
 
 def store_all(*refs):
@@ -728,7 +788,6 @@
         residue_mask,
         sequence_mask,
     ):
-        vmem = pl.BlockSpec(memory_space=pltpu.VMEM)
         ns = seq_devices
         chunk = C // ns
         outs = pl.pallas_call(
@@ -743,7 +802,7 @@
                 jax.ShapeDtypeStruct((C, C), F32),
             ),
             in_specs=[pl.BlockSpec(memory_space=pltpu.HBM)] * 10,
-            out_specs=(vmem,) * 7,
+            out_specs=(pl.BlockSpec(memory_space=pltpu.HBM),) * 7,
             scratch_shapes=[
                 pltpu.VMEM((nz, res + 8, W), F32),
                 pltpu.VMEM((ns, 1, 2 * W), F32),
@@ -766,9 +825,12 @@
                 pltpu.VMEM((ns, chunk, 2 * W), F32),
                 pltpu.VMEM((ns, chunk, 3 * W), F32),
                 pltpu.VMEM((ns, chunk, 3 * W), F32),
-                pltpu.VMEM((chunk, 5 * W), F32),
-                pltpu.VMEM((nz, chunk, 5 * W), F32),
-                pltpu.VMEM((ns, chunk, 5 * W), F32),
+                pltpu.VMEM((chunk, 3 * W), F32),
+                pltpu.VMEM((nz, chunk, 3 * W), F32),
+                pltpu.VMEM((ns, chunk, 3 * W), F32),
+                pltpu.VMEM((chunk, 2 * W), F32),
+                pltpu.VMEM((nz, chunk, 2 * W), F32),
+                pltpu.VMEM((ns, chunk, 2 * W), F32),
                 pltpu.VMEM((L, res, C), BF16),
                 pltpu.VMEM((L, res, C), BF16),
                 pltpu.VMEM((H, res, keys), BF16),
@@ -779,13 +841,21 @@
                 pltpu.VMEM((C, C), F32),
                 pltpu.VMEM((1, res), jnp.int32),
                 pltpu.VMEM((1, L), jnp.int32),
-                pltpu.SemaphoreType.DMA((9,)),
-                pltpu.SemaphoreType.DMA((9,)),
+                pltpu.SemaphoreType.DMA((11,)),
+                pltpu.SemaphoreType.DMA((11,)),
                 pltpu.SemaphoreType.DMA((3, PAIRS)),
                 pltpu.SemaphoreType.DMA((3, PAIRS)),
                 pltpu.SemaphoreType.DMA((10,)),
                 pltpu.SemaphoreType.DMA((8,)),
                 pltpu.SemaphoreType.DMA((8,)),
+                pltpu.VMEM((L, res, C), BF16),
+                pltpu.VMEM((H, block, res), F32),
+                pltpu.VMEM((2, C), F32),
+                pltpu.VMEM((C, 4 * C), F32),
+                pltpu.VMEM((C, C), F32),
+                pltpu.VMEM((C, 2 * C + 2 * DH), F32),
+                pltpu.VMEM((C, C), F32),
+                pltpu.SemaphoreType.DMA((7,)),
             ],
             compiler_params=pltpu.CompilerParams(
                 collective_id=0, has_side_effects=True, vmem_limit_bytes=64 * 1024 * 1024

time: 72.4 us -> 69.5 us (0.960)
  Pallas kernels: 71.6 us -> 68.6 us
    pallas_call x1, Pallas kernels: 69.9 us -> 67 us  [local(): pl.pallas_call(functools.partial(kernel, (ny, nx, nz)), out_shape=(jax.Sh...]
where the time goes in v3:
time: 69.5 us; the launch traced here: 69.3 us
  Pallas kernels  68.6 us (99%)
    pallas_call x1, Pallas kernels, local(): pl.pallas_call(functools.partial(kernel, (ny, nx, nz)), out_shape=(jax.Sh...  67 us
    pallas_call x1, Pallas kernels, finish(): pl.pallas_call(store_all, out_shape=tuple((jax.ShapeDtypeStruct(a.shape,...  1.65 us

profile of v3, /device:TPU:1, one launch (start us, length us, event | category | flops | bytes accessed | tf_op | source)
XLA Modules:
  0.0 69.3 jit_solution(15620405485342359745)
XLA Ops:
  0.6 67.0 %shard_map.153 = (bf16[2,64,64]{2,1,0:T(8,128)(2,1)}, f32[8,8,64]{2,1,0:T(8,128)}, f32[2,64]{1,0:T(2,128)}, f32[64,256]{1,0:T(8,128)}, f32[64,64]{1,0:T(8,128)}, /*index=5*/f32[64,144]{1,0:T(8,128)}, f32[64,64]{1,0:T(8,128)}) custom-call(bf16[2,64,64]{2,1,0:T(8,128)(2,1)} %align_hbm.1, bf16[2,64,64]{2,1,0:T(8,128)(2,1)} %cot_hbm.1, ...), custom_call_target="tpu_custom_call" | custom-call | tf_op jit(solution)/shard_map/pallas_call | solution.py:793
  67.6 1.6 %shard_map.154 = (bf16[2,64,64]{2,1,0:T(8,128)(2,1)}, f32[8,8,64]{2,1,0:T(8,128)}, f32[2,64]{1,0:T(2,128)}, f32[64,256]{1,0:T(8,128)}, f32[64,64]{1,0:T(8,128)}, /*index=5*/f32[64,144]{1,0:T(8,128)}, f32[64,64]{1,0:T(8,128)}) custom-call(bf16[2,64,64]{2,1,0:T(8,128)(2,1)} %get-tuple-element.21.refs_0_, f32[8,8,64]{2,1,0:T(8,128)} %get-tuple-element.22.refs_1_, ...), custom_call_target="tpu_custom_call" | custom-call | tf_op jit(solution)/shard_map/pallas_call | solution.py:758

commit v4 on v3

--- a/solution.py
+++ b/solution.py
@@ -131,6 +131,8 @@
     brecv,
     bias_t,
     exps,
+    exps_high,
+    exps_low,
     bias_s,
     core_r,
     x_s,
@@ -422,17 +424,33 @@
         pair = bias_ref[2 * p : 2 * p + 2].astype(F32).reshape(half, keys)
         bias_t[p] = pair.T
 
-    match = iota((W, wide), 0) // DH - iota((W, wide), 1) // res
+    mine = ones_where(iota((32, wide), 0) // DH == iota((32, wide), 1) // res)
+    nothing = jnp.zeros((32, wide), BF16)
+    group = iota((keys, W), 1) // 32
 
     def heads_apart(rows):
         flat = rows.T
         flat = jnp.concatenate([flat, flat, flat, flat], axis=1)
-        return [jnp.where(match == 4 * p, flat, 0.0) for p in range(PAIRS)]
-
-    queries_apart = heads_apart(queries)
-    query_terms = [split3(apart) for apart in queries_apart]
-
-    mine = ones_where(iota((32, wide), 0) // DH == iota((32, wide), 1) // res)
+        return [flat[32 * p : 32 * p + 32] * mine for p in range(PAIRS)]
+
+    def placed(part, p):
+        return jnp.concatenate([part if i == p else nothing for i in range(PAIRS)], axis=0)
+
+    def turns(part):
+        part = part.astype(F32)
+        return [part] + [pltpu.roll(part, 32 * i, 1) for i in range(1, PAIRS)]
+
+    def lanes_of(p, *parts):
+        found = parts[-1][(len(parts) - 1 - p) % PAIRS]
+        for i in reversed(range(len(parts) - 1)):
+            found = jnp.where(group == i, parts[i][(i - p) % PAIRS], found)
+        return found.astype(BF16)
+
+    query_parts = [split3(apart) for apart in heads_apart(queries)]
+    query_stacks = [
+        jnp.concatenate([q1, q2, q1, q2, q3, q1, nothing, nothing], axis=0)
+        for q1, q2, q3 in query_parts
+    ]
 
     def heads_together(apart):
         kept = apart * mine
@@ -463,13 +481,14 @@
     key_bias = jnp.concatenate(
         [MASKED * (mask_flat[:res, 8 * z : 8 * z + 1] - 1.0) for z in range(nz)], axis=0
     )
-    key_terms = split3(key_rows)
+    t1, t2, t3 = [turns(part) for part in split3(key_rows)]
     value_high, value_low = split2(value_flat)
 
     totals = []
     mixed = []
     for p in range(PAIRS):
-        scores = products(key_terms, query_terms[p])
+        key_stack = jnp.concatenate([lanes_of(p, t1, t1, t2, t2), lanes_of(p, t1, t3)], axis=1)
+        scores = dot1(key_stack, query_stacks[p])
         scores = scores + twice(bias_t[p]) + key_bias
         peak = jnp.max(scores, axis=0, keepdims=True)
         exponent = jnp.exp(scores - peak)
@@ -477,6 +496,8 @@
         inverse_total = 1.0 / jnp.sum(exponent, axis=0, keepdims=True)
         totals.append(inverse_total)
         eh, el = split2(exponent)
+        exps_high[p] = eh
+        exps_low[p] = el
         vh = value_high[32 * p : 32 * p + 32]
         vl = value_low[32 * p : 32 * p + 32]
         apart = dot1(vh, eh) + (dot1(vl, eh) + dot1(vh, el))
@@ -490,9 +511,6 @@
 
     key_flat = key_rows.T
     key_high, key_low = split2(key_flat)
-    v1, v2 = split2(value_rows)
-    hat_high, hat_low = split2(hat_all.T)
-    v12 = jnp.concatenate([v1, v2], axis=1)
 
     wait_all(grecv, 1, ns)
     top = grecv[:, 0, 0:W]
@@ -564,6 +582,10 @@
     to_seq(lambda j: pc_s.at[j], pc_r, 4)
     keep(pc_s, pc_r, me)
 
+    v1, v2 = [turns(part) for part in split2(value_rows)]
+    hat_high, hat_low = split2(hat_all.T)
+    value_stacks = [lanes_of(p, v1, v2, v1) for p in range(PAIRS)]
+
     wait_all(brecv, 3, ns)
     grad_middle = brecv[:, 0, :]
     grad_gated = dot(grad_middle, out_w, NT)
@@ -630,28 +652,46 @@
         gbias_ref[2 * p] = total[:, :res]
         gbias_ref[2 * p + 1] = total[:, res:]
 
-    grad_keys = jnp.zeros((keys, W), F32)
-    grad_values = jnp.zeros((keys, W), F32)
+    score_parts = []
+    value_parts = []
     grad_queries = []
     for p in range(PAIRS):
-        gh, gl = split2(grads_apart[p])
-        grad_weights = dot1(v12, jnp.concatenate([gh, gh], axis=0)) + dot1(v1, gl)
-        weights = exps[p] * totals[p]
-        inner = jnp.sum(weights * grad_weights, axis=0, keepdims=True)
-        grad_scores = weights * (grad_weights - inner)
+        gh, gl = split2(grads_apart[p] * totals[p])
+        grad_weights = dot1(value_stacks[p], jnp.concatenate([gh, gh, gl, nothing], axis=0))
+        exponent = exps[p]
+        inner = jnp.sum(exponent * grad_weights, axis=0, keepdims=True) * totals[p]
+        grad_scores = exponent * (grad_weights - inner)
         bias_s[p] = (grad_scores[:, :half] + grad_scores[:, half:]).reshape(
             ny, nx, 2, block, half
         )
         bias_core(p).start()
         sh, sl = split2(grad_scores)
-        wh, wl = split2(weights)
-        grad_keys = grad_keys + outer3((sh, sl), query_terms[p][:2])
-        grad_values = grad_values + outer3((wh, wl), (gh, gl))
+        score_parts.append((sh, sl))
+        value_parts.append((gh, gl))
         kh = key_high[32 * p : 32 * p + 32]
         kl = key_low[32 * p : 32 * p + 32]
         grad_queries.append(
             heads_together(dot1(kh, sh) + (dot1(kl, sh) + dot1(kh, sl)))
         )
+
+    empty = jnp.zeros((W, wide), BF16)
+
+    def outer_all(lefts, rights):
+        left = jnp.concatenate([part for pair in lefts for part in pair], axis=1)
+        highs = [placed(rh, p) for p, (rh, _) in enumerate(rights)]
+        lows = [placed(rl, p) for p, (_, rl) in enumerate(rights)]
+        right = jnp.concatenate(
+            [
+                jnp.concatenate([part for high in highs for part in (high, high)], axis=1),
+                jnp.concatenate([part for low in lows for part in (low, empty)], axis=1),
+            ],
+            axis=0,
+        )
+        both = dot1(left, right, NT)
+        return both[:, :W] + both[:, W:]
+
+    grad_keys = outer_all(score_parts, [parts[:2] for parts in query_parts])
+    grad_values = outer_all([(exps_high[p], exps_low[p]) for p in range(PAIRS)], value_parts)
 
     grad_memory = jnp.concatenate([grad_keys, grad_values], axis=1)
     grad_query = jnp.concatenate(grad_queries, axis=0).T * scaling
@@ -813,6 +853,8 @@
                 pltpu.VMEM((ns, 1, W), F32),
                 pltpu.VMEM((PAIRS, keys, half), F32),
                 pltpu.VMEM((PAIRS, keys, 2 * half), F32),
+                pltpu.VMEM((PAIRS, keys, 2 * half), BF16),
+                pltpu.VMEM((PAIRS, keys, 2 * half), BF16),
                 pltpu.VMEM((PAIRS, ny, nx, 2, block, half), F32),
                 pltpu.VMEM((PAIRS, ny, nx, block, half), F32),
                 pltpu.VMEM((PAIRS, nx, ny, block, half), F32),

time: 69.5 us -> 66.7 us (0.960)
  Pallas kernels: 68.6 us -> 65.9 us
    pallas_call x1, Pallas kernels: 67 us -> 64.3 us  [local(): pl.pallas_call(functools.partial(kernel, (ny, nx, nz)), out_shape=(jax.Sh...]
where the time goes in v4:
time: 66.7 us; the launch traced here: 66.6 us
  Pallas kernels  65.9 us (99%)
    pallas_call x1, Pallas kernels, local(): pl.pallas_call(functools.partial(kernel, (ny, nx, nz)), out_shape=(jax.Sh...  64.3 us
    pallas_call x1, Pallas kernels, finish(): pl.pallas_call(store_all, out_shape=tuple((jax.ShapeDtypeStruct(a.shape,...  1.65 us

profile of v4, /device:TPU:1, one launch (start us, length us, event | category | flops | bytes accessed | tf_op | source)
XLA Modules:
  0.0 66.6 jit_solution(5272502430815814625)
XLA Ops:
  0.6 64.3 %shard_map.153 = (bf16[2,64,64]{2,1,0:T(8,128)(2,1)}, f32[8,8,64]{2,1,0:T(8,128)}, f32[2,64]{1,0:T(2,128)}, f32[64,256]{1,0:T(8,128)}, f32[64,64]{1,0:T(8,128)}, /*index=5*/f32[64,144]{1,0:T(8,128)}, f32[64,64]{1,0:T(8,128)}) custom-call(bf16[2,64,64]{2,1,0:T(8,128)(2,1)} %align_hbm.1, bf16[2,64,64]{2,1,0:T(8,128)(2,1)} %cot_hbm.1, ...), custom_call_target="tpu_custom_call" | custom-call | tf_op jit(solution)/shard_map/pallas_call | solution.py:833
  64.9 1.6 %shard_map.154 = (bf16[2,64,64]{2,1,0:T(8,128)(2,1)}, f32[8,8,64]{2,1,0:T(8,128)}, f32[2,64]{1,0:T(2,128)}, f32[64,256]{1,0:T(8,128)}, f32[64,64]{1,0:T(8,128)}, /*index=5*/f32[64,144]{1,0:T(8,128)}, f32[64,64]{1,0:T(8,128)}) custom-call(bf16[2,64,64]{2,1,0:T(8,128)(2,1)} %get-tuple-element.21.refs_0_, f32[8,8,64]{2,1,0:T(8,128)} %get-tuple-element.22.refs_1_, ...), custom_call_target="tpu_custom_call" | custom-call | tf_op jit(solution)/shard_map/pallas_call | solution.py:798

commit v5 on v4

--- a/solution.py
+++ b/solution.py
@@ -65,6 +65,13 @@
     axis = dims[0][1][0]
     return dot1(
         jnp.concatenate(split2(values), axis=1), jnp.concatenate([ones, ones], axis=axis), dims
+    )
+
+
+def exact(values, fixed):
+    fixed = fixed.astype(BF16)
+    return dot1(
+        jnp.concatenate(split3(values), axis=1), jnp.concatenate([fixed, fixed, fixed], axis=0)
     )
 
 
@@ -363,15 +370,15 @@
     averaging = ones_where(iota((W, W), 0) // C == iota((W, W), 1) // C) * (1.0 / C)
 
     def layer_norm(values):
-        centred = values - dot(values, averaging)
-        spread = dot(centred * centred, averaging)
+        centred = values - exact(values, averaging)
+        spread = exact(centred * centred, averaging)
         inverse = lax.rsqrt(spread + EPSILON)
         return centred * inverse, inverse
 
     def layer_norm_back(grad_normed, gain, hat, inverse):
         scaled = grad_normed * gain
         rows = scaled.shape[0]
-        means = dot(jnp.concatenate([scaled, scaled * hat], axis=0), averaging)
+        means = exact(jnp.concatenate([scaled, scaled * hat], axis=0), averaging)
         return inverse * (scaled - means[:rows] - hat * means[rows:])
 
     hat_local, inverse_local = layer_norm(initial)
@@ -530,7 +537,7 @@
     key_col = projected[:, 0:W]
     value_col = projected[:, W : 2 * W]
     gate_col = jax.nn.sigmoid(projected[:, 2 * W :])
-    scores_col = dot(key_col * queries_col, head_sum) + MASKED * (present - 1.0)
+    scores_col = exact(key_col * queries_col, head_sum) + MASKED * (present - 1.0)
     peak_row = jnp.max(scores_col, axis=0, keepdims=True)
     peak_row = jnp.maximum(peak_row, jnp.concatenate([peak_row[:, C:], peak_row[:, :C]], axis=1))
     exp_col = jnp.exp(scores_col - peak_row)
@@ -538,7 +545,7 @@
     mixture_col = fold(jnp.sum(weights_col * value_col, axis=0, keepdims=True))
     grad_mixture_col = fold(jnp.sum(gate_col * grad_gated_col, axis=0, keepdims=True))
     grad_gate_col = grad_gated_col * mixture_col * gate_col * (1.0 - gate_col)
-    grad_weights_col = dot(value_col * grad_mixture_col, head_sum)
+    grad_weights_col = exact(value_col * grad_mixture_col, head_sum)
     inner_col = fold(jnp.sum(weights_col * grad_weights_col, axis=0, keepdims=True))
     grad_scores_col = weights_col * (grad_weights_col - inner_col)
     grad_query_col = fold(jnp.sum(grad_scores_col * key_col, axis=0, keepdims=True)) * scaling

time: 66.7 us -> 66.3 us (level)
  no operation moved by 1% of the time
where the time goes in v5:
time: 66.3 us; the launch traced here: 66.1 us
  Pallas kernels  65.5 us (99%)
    pallas_call x1, Pallas kernels, local(): pl.pallas_call(functools.partial(kernel, (ny, nx, nz)), out_shape=(jax.Sh...  63.8 us
    pallas_call x1, Pallas kernels, finish(): pl.pallas_call(store_all, out_shape=tuple((jax.ShapeDtypeStruct(a.shape,...  1.65 us

profile of v5, /device:TPU:1, one launch (start us, length us, event | category | flops | bytes accessed | tf_op | source)
XLA Modules:
  0.0 66.1 jit_solution(4523417472046321161)
XLA Ops:
  0.6 63.8 %shard_map.153 = (bf16[2,64,64]{2,1,0:T(8,128)(2,1)}, f32[8,8,64]{2,1,0:T(8,128)}, f32[2,64]{1,0:T(2,128)}, f32[64,256]{1,0:T(8,128)}, f32[64,64]{1,0:T(8,128)}, /*index=5*/f32[64,144]{1,0:T(8,128)}, f32[64,64]{1,0:T(8,128)}) custom-call(bf16[2,64,64]{2,1,0:T(8,128)(2,1)} %align_hbm.1, bf16[2,64,64]{2,1,0:T(8,128)(2,1)} %cot_hbm.1, ...), custom_call_target="tpu_custom_call" | custom-call | tf_op jit(solution)/shard_map/pallas_call | solution.py:840
  64.5 1.6 %shard_map.154 = (bf16[2,64,64]{2,1,0:T(8,128)(2,1)}, f32[8,8,64]{2,1,0:T(8,128)}, f32[2,64]{1,0:T(2,128)}, f32[64,256]{1,0:T(8,128)}, f32[64,64]{1,0:T(8,128)}, /*index=5*/f32[64,144]{1,0:T(8,128)}, f32[64,64]{1,0:T(8,128)}) custom-call(bf16[2,64,64]{2,1,0:T(8,128)(2,1)} %get-tuple-element.21.refs_0_, f32[8,8,64]{2,1,0:T(8,128)} %get-tuple-element.22.refs_1_, ...), custom_call_target="tpu_custom_call" | custom-call | tf_op jit(solution)/shard_map/pallas_call | solution.py:805
